TPU v7x, 128 devices: a whole 4x4x4 slice. The times are simulated.
128 devices in a mesh: dp: 2 (over core), mx: 16 (over y, x), my: 4 (over z).
Axes of the slice: x: 4, y: 4, z: 4, core: 2. Of those that a mesh axis runs over, the one named last changes fastest.
Arguments:
- features: bfloat16 [1024, 6144], P('dp', ('mx', 'my')), may hold values from -9 to 9
- w_qkv: bfloat16 [6144, 24, 384], P('mx', 'my'), may hold values from -0.078125 to 0.078125
- w_up: bfloat16 [6144, 12288], P('mx', 'my'), may hold values from -0.078125 to 0.078125
- w_out: bfloat16 [24, 128, 6144], P('my', None, 'mx'), may hold values from -0.109375 to 0.109375
- w_down: bfloat16 [12288, 6144], P('my', 'mx'), may hold values from -0.0546875 to 0.0546875
- grad_out: bfloat16 [1024, 6144], P('dp', ('mx', 'my')), may hold values from -6 to 6
Outputs:
- layer_out: bfloat16 [1024, 6144], P('dp', ('mx', 'my'))
- grad_in: bfloat16 [1024, 6144], P('dp', ('mx', 'my'))
- grad_qkv: float32 [6144, 24, 384], P(('mx', 'dp'), 'my')
- grad_up: float32 [6144, 12288], P(('mx', 'dp'), 'my')
- grad_attn_out: float32 [24, 128, 6144], P('my', None, ('mx', 'dp'))
- grad_down: float32 [12288, 6144], P('my', ('mx', 'dp'))
All inputs are finite; a program needn't handle non-finite values.
Results may differ from a plain program's by a relative error of at most 0.0094.
Values may be sent and summed in bfloat16 or wider, within the bound.
A program may use at most 128 MiB of HBM per device.

v0:
```python
import math

import jax
import jax.numpy as jnp
from jax import lax
from jax.sharding import PartitionSpec as P

D = 6144


epsilon = 1e-06


def row_stats(totals, entries):
    average = totals[0] / entries
    spread = totals[1] / entries - average * average
    return (average, lax.rsqrt(spread + epsilon))


def head_norm(values):
    average = jnp.mean(values, -1, keepdims=True)
    spread = jnp.mean(values * values, -1, keepdims=True) - average * average
    inverse = lax.rsqrt(spread + epsilon)
    return ((values - average) * inverse, inverse)


def head_norm_back(gradient, normal, inverse):
    first_mean = jnp.mean(gradient, -1, keepdims=True)
    second_mean = jnp.mean(gradient * normal, -1, keepdims=True)
    return inverse * (gradient - first_mean - normal * second_mean)


def gelu_value(values):
    return 0.5 * values * (1.0 + jax.scipy.special.erf(values / math.sqrt(2.0)))


def gelu_slope(values):
    return 0.5 * (1.0 + jax.scipy.special.erf(values / math.sqrt(2.0))) + values * jnp.exp(
        -0.5 * values * values
    ) / math.sqrt(2.0 * math.pi)


def contract_first(left_side, right_side):
    return lax.dot_general(
        left_side, right_side, (((0,), (0,)), ((), ())), preferred_element_type=jnp.float32
    )


def contract_last(left_side, right_side):
    return lax.dot_general(
        left_side, right_side, (((1,), (1,)), ((), ())), preferred_element_type=jnp.float32
    )


def on_device(features, w_qkv, w_up, w_out, w_down, grad_out):
    tokens = features.shape[0]
    block_rows = tokens // lax.axis_size("mx")
    heads = w_qkv.shape[1]
    head_size = w_qkv.shape[2] // 3
    attn_width = heads * head_size
    qkv_width = 3 * attn_width
    factor = 1.0 / math.sqrt(head_size)
    qkv_flat = w_qkv.reshape(w_qkv.shape[0], qkv_width)
    out_flat = w_out.reshape(attn_width, w_out.shape[2])
    own = features.astype(jnp.float32)
    gathered = lax.all_gather(features, "my", axis=1, tiled=True).astype(jnp.float32)
    totals = lax.psum((jnp.sum(gathered, 1), jnp.sum(gathered * gathered, 1)), "mx")
    average, inverse = row_stats(totals, D)
    normed = ((gathered - average[:, None]) * inverse[:, None]).astype(jnp.bfloat16)
    normal_own = (own - average[:, None]) * inverse[:, None]
    part_rows = normed
    projected = lax.psum_scatter(
        jnp.concatenate(
            [
                jnp.dot(part_rows, qkv_flat, preferred_element_type=jnp.float32),
                jnp.dot(part_rows, w_up, preferred_element_type=jnp.float32),
            ],
            1,
        ),
        "mx",
        scatter_dimension=0,
        tiled=True,
    )
    joined = projected[:, :qkv_width].reshape(block_rows, heads, 3 * head_size)
    hidden_pre = projected[:, qkv_width:]
    query_norm, query_inv = head_norm(joined[:, :, :head_size])
    key_norm, key_inv = head_norm(joined[:, :, head_size : 2 * head_size])
    query_b = query_norm.astype(jnp.bfloat16)
    key_b = key_norm.astype(jnp.bfloat16)
    value_b = joined[:, :, 2 * head_size :].astype(jnp.bfloat16)
    hidden_act = gelu_value(hidden_pre).astype(jnp.bfloat16)
    keys_all, values_all = (
        lax.all_gather(key_b, "mx", axis=0, tiled=True),
        lax.all_gather(value_b, "mx", axis=0, tiled=True),
    )
    scores = (
        jnp.einsum("qhc,khc->hqk", query_b, keys_all, preferred_element_type=jnp.float32) * factor
    )
    raised = jnp.exp(scores)
    probs = raised / jnp.sum(raised, -1, keepdims=True)
    probs_b = probs.astype(jnp.bfloat16)
    attended = jnp.einsum("hqk,khc->qhc", probs_b, values_all, preferred_element_type=jnp.float32)
    attended = attended.astype(jnp.bfloat16).reshape(block_rows, attn_width)
    attended_all, hidden_all = (
        lax.all_gather(attended, "mx", axis=0, tiled=True),
        lax.all_gather(hidden_act, "mx", axis=0, tiled=True),
    )
    partial_sum = jnp.dot(attended_all, out_flat, preferred_element_type=jnp.float32) + jnp.dot(
        hidden_all, w_down, preferred_element_type=jnp.float32
    )
    branch_sum = lax.psum_scatter(partial_sum, "my", scatter_dimension=1, tiled=True)
    layer_out = (own + branch_sum).astype(jnp.bfloat16)
    grad_wide = lax.all_gather(grad_out, "my", axis=1, tiled=True)
    part_rows = grad_wide
    back_mixed = lax.psum_scatter(
        jnp.concatenate([contract_last(part_rows, out_flat), contract_last(part_rows, w_down)], 1),
        "mx",
        scatter_dimension=0,
        tiled=True,
    )
    grad_attended = (
        back_mixed[:, :attn_width].astype(jnp.bfloat16).reshape(block_rows, heads, head_size)
    )
    grad_hidden = back_mixed[:, attn_width:] * gelu_slope(hidden_pre)
    grad_probs = jnp.einsum(
        "qhc,khc->hqk", grad_attended, values_all, preferred_element_type=jnp.float32
    )
    row_dot = jnp.sum(probs * grad_probs, -1, keepdims=True)
    grad_scores = (probs * (grad_probs - row_dot)).astype(jnp.bfloat16)
    grad_query = (
        jnp.einsum("hqk,khc->qhc", grad_scores, keys_all, preferred_element_type=jnp.float32)
        * factor
    )
    key_part = (
        jnp.einsum("hqk,qhc->khc", grad_scores, query_b, preferred_element_type=jnp.float32)
        * factor
    )
    value_part = jnp.einsum(
        "hqk,qhc->khc", probs_b, grad_attended, preferred_element_type=jnp.float32
    )
    key_grad, value_grad = (
        lax.psum_scatter(key_part, "mx", scatter_dimension=0, tiled=True),
        lax.psum_scatter(value_part, "mx", scatter_dimension=0, tiled=True),
    )
    grad_joined = jnp.concatenate(
        [
            head_norm_back(grad_query, query_norm, query_inv),
            head_norm_back(key_grad, key_norm, key_inv),
            value_grad,
        ],
        -1,
    )
    grad_joined = grad_joined.astype(jnp.bfloat16).reshape(block_rows, qkv_width)
    grad_hidden_b = grad_hidden.astype(jnp.bfloat16)
    joined_all, hidden_grad_all = (
        lax.all_gather(grad_joined, "mx", axis=0, tiled=True),
        lax.all_gather(grad_hidden_b, "mx", axis=0, tiled=True),
    )
    input_part = contract_last(joined_all, qkv_flat) + contract_last(hidden_grad_all, w_up)
    grad_normed = lax.psum_scatter(input_part, "my", scatter_dimension=1, tiled=True)
    back_totals = lax.psum(
        (jnp.sum(grad_normed, 1), jnp.sum(grad_normed * normal_own, 1)), ("mx", "my")
    )
    correction = (
        grad_normed - back_totals[0][:, None] / D - normal_own * (back_totals[1][:, None] / D)
    )
    grad_in = (grad_out.astype(jnp.float32) + inverse[:, None] * correction).astype(jnp.bfloat16)
    grad_qkv, grad_up = (
        lax.psum_scatter(contract_first(normed, joined_all), "dp", scatter_dimension=0, tiled=True),
        lax.psum_scatter(
            contract_first(normed, hidden_grad_all), "dp", scatter_dimension=0, tiled=True
        ),
    )
    grad_attn_out, grad_down = (
        lax.psum_scatter(
            contract_first(attended_all, grad_wide), "dp", scatter_dimension=1, tiled=True
        ),
        lax.psum_scatter(
            contract_first(hidden_all, grad_wide), "dp", scatter_dimension=1, tiled=True
        ),
    )
    grad_qkv = grad_qkv.reshape(grad_qkv.shape[0], heads, 3 * head_size)
    grad_attn_out = grad_attn_out.reshape(heads, head_size, grad_attn_out.shape[1])
    return (layer_out, grad_in, grad_qkv, grad_up, grad_attn_out, grad_down)


def solution(mesh):
    in_specs = (
        P("dp", ("mx", "my")),
        P("mx", "my", None),
        P("mx", "my"),
        P("my", None, "mx"),
        P("my", "mx"),
        P("dp", ("mx", "my")),
    )
    out_specs = (
        P("dp", ("mx", "my")),
        P("dp", ("mx", "my")),
        P(("mx", "dp"), "my", None),
        P(("mx", "dp"), "my"),
        P("my", None, ("mx", "dp")),
        P("my", ("mx", "dp")),
    )
    return jax.shard_map(
        on_device, mesh=mesh, in_specs=in_specs, out_specs=out_specs, check_vma=False
    )
```

profile of v0, /device:TPU:0, one launch (start us, length us, event | category | flops | bytes accessed | tf_op | source)
XLA Modules:
  0.0 795.8 jit_solution(7981304287661218017)
XLA Ops:
  7.2 14.2 %all_gather.24 = bf16[512,384]{0,1:T(8,128)(2,1)S(1)} all-gather(bf16[512,96]{0,1:T(8,128)(2,1)} %param.6), channel_id=1, replica_groups=mesh['dp'=2,'mx'=16,'my'=4] {'my'}, dimensions={1}, use_global_device_ids=true | all-gather | bytes 491520 | tf_op jit(solution)/shard_map/all_gather | solution.py:66
  25.3 40.6 %all-reduce.1 = (f32[512]{0:T(512)S(1)}, f32[512]{0:T(512)S(1)}) all-reduce(f32[512]{0:T(512)S(1)} %get-tuple-element.19, f32[512]{0:T(512)S(1)} %get-tuple-element.18), channel_id=1, replica_groups=mesh['dp'=2,'mx'=16,'my'=4] {'mx'}, use_global_device_ids=true, to_apply=%region_3.0 | all-reduce | flops 1024 | bytes 8192 | tf_op jit(solution)/shard_map/psum | solution.py:67
  66.0 5.1 fusion.29
  71.1 4.4 fusion.27
  75.5 9.0 %pad_maximum_fusion = f32[512,5376]{1,0:T(8,128)} fusion(f32[512,3072]{1,0:T(8,128)} %fusion.27, f32[512,2304]{1,0:T(8,128)} %fusion.29), kind=kLoop, calls=%fused_computation | loop fusion | flops 2752512 | bytes 22020096 | tf_op jit(solution)/shard_map/concatenate | solution.py:73
  85.4 12.7 %all_gather.29 = bf16[512,384]{0,1:T(8,128)(2,1)S(1)} all-gather(bf16[512,96]{0,1:T(8,128)(2,1)S(1)} %copy-done.9), channel_id=1, replica_groups=mesh['dp'=2,'mx'=16,'my'=4] {'my'}, dimensions={1}, use_global_device_ids=true | all-gather | bytes 491520 | tf_op jit(solution)/shard_map/all_gather | solution.py:113
  105.5 66.6 %reduce-scatter.11.cloned.1.call-done = f32[32,5376]{1,0:T(8,128)} async-done(((f32[512,5376]{1,0:T(8,128)}), f32[32,5376]{1,0:T(8,128)}) %reduce-scatter.11.cloned.1.call-update) | async-done | bytes 688144 | tf_op jit(solution)/shard_map/reduce_scatter | solution.py:72
  175.7 26.7 %all_gather.26 = bf16[512,6,128]{2,0,1:T(8,128)(2,1)} all-gather(bf16[32,6,128]{2,0,1:T(8,128)(2,1)S(1)} %fusion.34), channel_id=1, replica_groups=mesh['dp'=2,'mx'=16,'my'=4] {'mx'}, dimensions={0}, use_global_device_ids=true | all-gather | bytes 835584 | tf_op jit(solution)/shard_map/all_gather | solution.py:93
  202.4 26.4 %all_gather.25 = bf16[512,6,128]{2,0,1:T(8,128)(2,1)} all-gather(bf16[32,6,128]{2,0,1:T(8,128)(2,1)S(1)} %copy.68), channel_id=1, replica_groups=mesh['dp'=2,'mx'=16,'my'=4] {'mx'}, dimensions={0}, use_global_device_ids=true | all-gather | bytes 835584 | tf_op jit(solution)/shard_map/all_gather | solution.py:94
  228.8 32.2 %reduce-scatter.15.cloned.1.call-done = f32[32,3840]{1,0:T(8,128)} async-done(((f32[512,3840]{1,0:T(8,128)}), f32[32,3840]{1,0:T(8,128)}) %reduce-scatter.15.cloned.1.call-update) | async-done | bytes 491536 | tf_op jit(solution)/shard_map/reduce_scatter | solution.py:115
  276.0 67.2 %reduce-scatter.17.cloned.1.call-done = f32[32,6,128]{2,0,1:T(8,128)} async-done(((f32[512,6,128]{2,0,1:T(8,128)}), f32[32,6,128]{2,0,1:T(8,128)}) %reduce-scatter.17.cloned.1.call-update) | async-done | bytes 98320 | tf_op jit(solution)/shard_map/reduce_scatter | solution.py:142
  344.4 75.4 %reduce-scatter.19.cloned.1.call-done = f32[32,6,128]{2,0,1:T(8,128)} async-done(((f32[512,6,128]{2,0,1:T(8,128)}), f32[32,6,128]{2,0,1:T(8,128)}) %reduce-scatter.19.cloned.1.call-update) | async-done | bytes 98320 | tf_op jit(solution)/shard_map/reduce_scatter | solution.py:143
  427.9 24.4 %all_gather.27 = bf16[512,768]{1,0:T(8,128)(2,1)S(1)} all-gather(bf16[32,768]{1,0:T(8,128)(2,1)S(1)} %bitcast.72), channel_id=1, replica_groups=mesh['dp'=2,'mx'=16,'my'=4] {'mx'}, dimensions={0}, use_global_device_ids=true | all-gather | bytes 835584 | tf_op jit(solution)/shard_map/all_gather | solution.py:105
  454.8 13.9 %all-gather.6.cloned.1.call-done = bf16[512,2304]{1,0:T(8,128)(2,1)} async-done(((bf16[32,2304]{1,0:T(8,128)(2,1)}), bf16[512,2304]{1,0:T(8,128)(2,1)}) %all-gather.6.cloned.1.call-update) | async-done | bytes 2359312 | tf_op jit(solution)/shard_map/all_gather | solution.py:156
  468.7 4.2 fusion.52
  472.9 45.5 %all-gather.8.cloned.1.call-done = bf16[512,3072]{1,0:T(8,128)(2,1)} async-done(((bf16[32,3072]{1,0:T(8,128)(2,1)}), bf16[512,3072]{1,0:T(8,128)(2,1)}) %all-gather.8.cloned.1.call-update) | async-done | bytes 3145744 | tf_op jit(solution)/shard_map/all_gather | solution.py:157
  518.4 4.4 convolution_add_fusion.1
  522.8 44.5 %all-gather.4.cloned.1.call-done = bf16[512,3072]{1,0:T(8,128)(2,1)} async-done(((bf16[32,3072]{1,0:T(8,128)(2,1)}), bf16[512,3072]{1,0:T(8,128)(2,1)}) %all-gather.4.cloned.1.call-update) | async-done | bytes 3145744 | tf_op jit(solution)/shard_map/all_gather | solution.py:106
  567.3 4.1 fusion.49
  573.0 4.5 fusion.25
  577.6 5.5 fusion.23
  583.1 5.4 fusion.54
  590.6 16.6 %reduce-scatter.21.cloned.1.call-done = f32[512,96]{0,1:T(8,128)} async-done(((f32[512,384]{0,1:T(8,128)}), f32[512,96]{0,1:T(8,128)}) %reduce-scatter.21.cloned.1.call-update) | async-done | bytes 196624 | tf_op jit(solution)/shard_map/reduce_scatter | solution.py:160
  608.1 176.6 %all-reduce = (f32[512]{0:T(512)S(1)}, f32[512]{0:T(512)S(1)}) all-reduce(f32[512]{0:T(512)S(1)} %get-tuple-element.21, f32[512]{0:T(512)S(1)} %get-tuple-element.20), channel_id=1, replica_groups=mesh['dp'=2,'mx'=16,'my'=4] {'mx','my'}, use_global_device_ids=true, to_apply=%region_23.0 | all-reduce | flops 1024 | bytes 8192 | tf_op jit(solution)/shard_map/psum | solution.py:161
  (98 shorter events, 51.5 us)
Async XLA Ops:
  7.2 63.9 %copy-start = (bf16[384,3072]{1,0:T(8,128)(2,1)S(1)}, bf16[384,3072]{1,0:T(8,128)(2,1)}, u32[]{:S(2)}) copy-start(bf16[384,3072]{1,0:T(8,128)(2,1)} %param.8) | copy-start | bytes 7077892
  7.2 165.0 %reduce-scatter.11.cloned.1.call-start = ((), (), s32[]{:S(2)}) async-start(), calls=%async_computation.10 | async-start | bytes 11698176 | tf_op jit(solution)/shard_map/reduce_scatter | solution.py:72
  84.5 0.9 copy-start.9
  84.6 176.4 %reduce-scatter.15.cloned.1.call-start = ((), (), s32[]{:S(2)}) async-start(), calls=%async_computation.13 | async-start | bytes 8355840 | tf_op jit(solution)/shard_map/reduce_scatter | solution.py:115
  85.4 14.4 %copy-start.6 = (bf16[3072,384]{1,0:T(8,128)(2,1)S(1)}, bf16[3072,384]{1,0:T(8,128)(2,1)}, u32[]{:S(2)}) copy-start(bf16[3072,384]{1,0:T(8,128)(2,1)} %param.10) | copy-start | bytes 7077892
  105.5 237.7 %reduce-scatter.17.cloned.1.call-start = ((), (), s32[]{:S(2)}) async-start(), calls=%async_computation.14 | async-start | bytes 1671168 | tf_op jit(solution)/shard_map/reduce_scatter | solution.py:142
  174.9 0.8 copy-start.4
  175.2 53.5 %copy-start.11 = (f32[32,6]{0,1:T(8,128)}, f32[32,6]{0,1:T(8,128)S(1)}, u32[]{:S(2)}) copy-start(f32[32,6]{0,1:T(8,128)S(1)} %get-tuple-element.42) | copy-start | bytes 2308
  175.2 53.5 %copy-start.12 = (f32[32,6]{0,1:T(8,128)}, f32[32,6]{0,1:T(8,128)S(1)}, u32[]{:S(2)}) copy-start(f32[32,6]{0,1:T(8,128)S(1)} %get-tuple-element.43) | copy-start | bytes 2308
  270.1 149.6 %reduce-scatter.19.cloned.1.call-start = ((), (), s32[]{:S(2)}) async-start(), calls=%async_computation.15 | async-start | bytes 1671168 | tf_op jit(solution)/shard_map/reduce_scatter | solution.py:143
  272.7 196.0 %all-gather.6.cloned.1.call-start = ((), (), s32[]{:S(2)}) async-start(), calls=%async_computation.16 | async-start | bytes 2506752 | tf_op jit(solution)/shard_map/all_gather | solution.py:156
  423.4 95.0 %all-gather.8.cloned.1.call-start = ((), (), s32[]{:S(2)}) async-start(), calls=%async_computation.17 | async-start | bytes 3342336 | tf_op jit(solution)/shard_map/all_gather | solution.py:157
  425.5 141.8 %all-gather.4.cloned.1.call-start = ((), (), s32[]{:S(2)}) async-start(), calls=%async_computation.11 | async-start | bytes 3342336 | tf_op jit(solution)/shard_map/all_gather | solution.py:106
  426.2 162.4 %reduce-scatter.27.cloned.1.call-start = ((), (), s32[]{:S(2)}) async-start(), calls=%async_computation.21 | async-start | bytes 1769472 | tf_op jit(solution)/shard_map/reduce_scatter | solution.py:175
  452.3 0.9 copy-start.1
  454.7 152.4 %reduce-scatter.21.cloned.1.call-start = ((), (), s32[]{:S(2)}) async-start(), calls=%async_computation.18 | async-start | bytes 983040 | tf_op jit(solution)/shard_map/reduce_scatter | solution.py:160
  522.8 261.9 %reduce-scatter.13.cloned.1.call-start = ((), (), s32[]{:S(2)}) async-start(), calls=%async_computation.12 | async-start | bytes 983040 | tf_op jit(solution)/shard_map/reduce_scatter | solution.py:111
  567.3 4.2 copy-start.2
  567.3 4.2 copy-start.5
  572.9 213.6 %reduce-scatter.23.cloned.1.call-start = ((), (), s32[]{:S(2)}) async-start(), calls=%async_computation.19 | async-start | bytes 5308416 | tf_op jit(solution)/shard_map/reduce_scatter | solution.py:169
  577.5 211.8 %reduce-scatter.25.cloned.1.call-start = ((), (), s32[]{:S(2)}) async-start(), calls=%async_computation.20 | async-start | bytes 7077888 | tf_op jit(solution)/shard_map/reduce_scatter | solution.py:170
  583.1 206.2 %reduce-scatter.29.cloned.1.call-start = ((), (), s32[]{:S(2)}) async-start(), calls=%async_computation.22 | async-start | bytes 7077888 | tf_op jit(solution)/shard_map/reduce_scatter | solution.py:178
  588.6 18.6 %copy-start.8 = (bf16[512,96]{0,1:T(8,128)(2,1)S(1)}, bf16[512,96]{0,1:T(8,128)(2,1)}, u32[]{:S(2)}) copy-start(bf16[512,96]{0,1:T(8,128)(2,1)} %param.6) | copy-start | bytes 294916
  588.6 196.1 %copy-start.10 = (bf16[512,96]{0,1:T(8,128)(2,1)S(1)}, bf16[512,96]{0,1:T(8,128)(2,1)}, u32[]{:S(2)}) copy-start(bf16[512,96]{0,1:T(8,128)(2,1)} %param.11) | copy-start | bytes 294916
  (2 other events, 1.3 us)
Sparse Core Ops, SparseCore 0:
  84.7 87.4 reduce-scatter.10
  176.1 84.8 reduce-scatter.14
  270.3 72.8 reduce-scatter.16
  346.9 72.8 reduce-scatter.18
  423.5 45.1 all-gather.5
  471.3 47.0 all-gather.7
  520.5 46.7 all-gather.3
  569.7 10.2 reduce-scatter.26
  583.0 24.0 reduce-scatter.20
  609.5 22.3 reduce-scatter.12
  634.4 13.6 reduce-scatter.22
  650.9 16.6 reduce-scatter.24
  670.7 16.6 reduce-scatter.28
where the time goes:
time: 797 us; the launch traced here: 796 us
  waiting for transfers between devices  363 us (46%)
  blocking collectives  322 us (40%)
  matrix products  56.8 us (7%)
  other arithmetic  25 us (3%)
  local copies, waits for them, and re-layouts  14.7 us (2%)
  between operations  14.2 us (2%)
    psum x1, blocking collectives, on_device(): lax.psum((jnp.sum(grad_normed, 1), jnp.sum(grad_normed * normal_own, 1)),...  177 us
    reduce_scatter x1, waiting for transfers between devices, on_device(): lax.psum_scatter(value_part, 'mx', scatter_dimension=0, tiled=True)  75.4 us
    reduce_scatter x1, waiting for transfers between devices, on_device(): lax.psum_scatter(key_part, 'mx', scatter_dimension=0, tiled=True)  67.2 us
    reduce_scatter x1, waiting for transfers between devices, on_device(): lax.psum_scatter(jnp.concatenate([jnp.dot(part_rows, qkv_flat, preferred_...  66.6 us
    all_gather x1, waiting for transfers between devices, on_device(): lax.all_gather(grad_hidden_b, 'mx', axis=0, tiled=True)  45.5 us
    all_gather x1, waiting for transfers between devices, on_device(): lax.all_gather(hidden_act, 'mx', axis=0, tiled=True)  44.5 us
    psum x1, blocking collectives, on_device(): lax.psum((jnp.sum(gathered, 1), jnp.sum(gathered * gathered, 1)), 'mx')  40.6 us
    reduce_scatter x1, waiting for transfers between devices, on_device(): lax.psum_scatter(jnp.concatenate([contract_last(part_rows, out_flat), con...  32.2 us
  transfers between devices with their start and end apart: 13, of which 8 were waited for; matrix products, arithmetic and copies ran while one was open for 7% of the time, Pallas kernels for 0%

commit v1 on v0

v1 whole, which is shorter than its diff:
```python
import math

import jax
import jax.numpy as jnp
from jax import lax
from jax.experimental import pallas as pl
from jax.experimental.pallas import tpu as pltpu
from jax.sharding import PartitionSpec as P

D = 6144
EPS = 1e-06
F32 = jnp.float32
BF16 = jnp.bfloat16
MESH = pl.DeviceIdType.MESH
HEADS = 6
HS = 128
TOK = 512
OWN = 32
BLK = 384
ZC = 96
FACTOR = 1.0 / math.sqrt(HS)
N_SEMS = 300
TILE = 768


def mm(a, b):
    return lax.dot_general(a, b, (((1,), (0,)), ((), ())), preferred_element_type=F32)


def mmt(a, b):
    return lax.dot_general(a, b, (((1,), (1,)), ((), ())), preferred_element_type=F32)


def mtm(a, b):
    return lax.dot_general(a, b, (((0,), (0,)), ((), ())), preferred_element_type=F32)


def gelu_value(values):
    return 0.5 * values * (1.0 + lax.erf(values / math.sqrt(2.0)))


def gelu_slope(values):
    return 0.5 * (1.0 + lax.erf(values / math.sqrt(2.0))) + values * jnp.exp(
        -0.5 * values * values
    ) / math.sqrt(2.0 * math.pi)


def head_norm(values):
    average = jnp.mean(values, -1, keepdims=True)
    spread = jnp.mean(values * values, -1, keepdims=True) - average * average
    inverse = lax.rsqrt(spread + EPS)
    return ((values - average) * inverse, inverse)


def head_norm_back(gradient, normal, inverse):
    first_mean = jnp.mean(gradient, -1, keepdims=True)
    second_mean = jnp.mean(gradient * normal, -1, keepdims=True)
    return inverse * (gradient - first_mean - normal * second_mean)


def placed(rows, columns, shift):
    row = lax.broadcasted_iota(jnp.int32, (rows, columns), 0)
    column = lax.broadcasted_iota(jnp.int32, (rows, columns), 1)
    return jnp.where(row + shift == column, 1.0, 0.0).astype(BF16)


def add_to(ref, more):
    ref[...] = (ref[...].astype(F32) + more[...].astype(F32)).astype(BF16)


class Links:
    def __init__(self, send, recv):
        self.send_sems, self.recv_sems, self.count, self.started = send, recv, 0, []
        mx = lax.axis_index("mx")
        self.x, self.y = lax.rem(mx, 4), lax.div(mx, 4)
        self.z, self.core = lax.axis_index("my"), lax.axis_index("dp")
        x, y, z = self.x, self.y, self.z
        self.xs = [lax.rem(x + i, 4) for i in range(4)]
        self.ys = [lax.rem(y + i, 4) for i in range(4)]
        self.zs = [lax.rem(z + i, 4) for i in range(4)]
        self.xd = [{"mx": y * 4 + v} for v in self.xs]
        self.yd = [{"mx": v * 4 + x} for v in self.ys]
        self.zd = [{"my": v} for v in self.zs]
        self.cd = {"dp": 1 - self.core}

    def send(self, src, dst, device):
        i = self.count
        self.count += 1
        copy = pltpu.make_async_remote_copy(
            src_ref=src,
            dst_ref=dst,
            send_sem=self.send_sems.at[i],
            recv_sem=self.recv_sems.at[i],
            device_id=device,
            device_id_type=MESH,
        )
        copy.start()
        self.started.append(copy)
        return copy

    def barrier(self):
        sem = pltpu.get_barrier_semaphore()
        peers = self.xd[1:] + self.yd[1:] + self.zd[1:] + [self.cd]
        for peer in peers:
            pl.semaphore_signal(sem, inc=1, device_id=peer, device_id_type=MESH)
        pl.semaphore_wait(sem, len(peers))


def rows_of(start, size):
    return pl.ds(pl.multiple_of(start, 16), size)


class RingSum:
    def __init__(self, links, ring, devices, chunk, first, second, opp, near):
        self.k, self.ring, self.dev = links, ring, devices
        self.chunk, self.first, self.second, self.opp, self.near = chunk, first, second, opp, near

    def start(self):
        far = self.chunk(self.ring[2])
        self.to_left = self.k.send(self.first(far), self.opp.at[1], self.dev[3])
        self.to_right = self.k.send(self.second(far), self.opp.at[0], self.dev[1])

    def middle(self):
        left, right = self.chunk(self.ring[3]), self.chunk(self.ring[1])
        self.to_left.wait_recv()
        add_to(self.first(left), self.opp.at[1])
        self.near_left = self.k.send(left, self.near.at[1], self.dev[3])
        self.to_right.wait_recv()
        add_to(self.second(right), self.opp.at[0])
        self.near_right = self.k.send(right, self.near.at[0], self.dev[1])

    def arrive(self):
        self.near_left.wait_recv()
        self.near_right.wait_recv()

    def total(self):
        self.arrive()
        own = self.chunk(self.ring[0])
        return own[...].astype(F32) + self.near[0].astype(F32) + self.near[1].astype(F32)

    def fold(self):
        own = self.chunk(self.ring[0])
        own[...] = self.total().astype(BF16)


class RingGather:
    def __init__(self, links, ring, devices, chunk, first, second):
        self.k, self.ring, self.dev = links, ring, devices
        self.chunk, self.first, self.second = chunk, first, second

    def start(self):
        own = self.chunk(self.ring[0])
        self.to_left = self.k.send(own, own, self.dev[3])
        self.to_right = self.k.send(own, own, self.dev[1])

    def middle(self):
        self.to_right.wait_recv()
        part = self.first(self.chunk(self.ring[3]))
        self.on_right = self.k.send(part, part, self.dev[1])
        self.to_left.wait_recv()
        part = self.second(self.chunk(self.ring[1]))
        self.on_left = self.k.send(part, part, self.dev[3])

    def finish(self):
        self.on_right.wait_recv()
        self.on_left.wait_recv()


def split_rows(n):
    return (lambda r: r.at[pl.ds(0, n)]), (lambda r: r.at[pl.ds(n, n)])


class Scatter:
    def __init__(self, links, part, bufs):
        k, h = links, part.shape[2] // 2
        a, b = pl.ds(0, h), pl.ds(h, h)
        a1o, a1n, b1o, b1n, o2, n2 = bufs
        x, y = k.x, k.y
        self.a1 = RingSum(k, k.ys, k.yd, lambda j: part.at[j, :, a], *split_rows(64), a1o, a1n)
        self.b1 = RingSum(
            k, k.xs, k.xd, lambda j: part.at[:, rows_of(j * 32, 32), b], *split_rows(2), b1o, b1n
        )
        self.a2 = RingSum(
            k,
            k.xs,
            k.xd,
            lambda j: part.at[y, rows_of(j * 32, 32), a],
            *split_rows(16),
            o2.at[0],
            n2.at[0],
        )
        self.b2 = RingSum(
            k,
            k.ys,
            k.yd,
            lambda j: part.at[j, rows_of(x * 32, 32), b],
            *split_rows(16),
            o2.at[1],
            n2.at[1],
        )

    def s1(self):
        self.a1.start()
        self.b1.start()

    def s2(self):
        self.a1.middle()
        self.b1.middle()

    def s3(self):
        self.a1.fold()
        self.a2.start()
        self.b1.fold()
        self.b2.start()

    def s4(self):
        self.a2.middle()
        self.b2.middle()

    def fin(self):
        return self.a2.total(), self.b2.total()


def scatter_scratch(c):
    h = c // 2
    return [
        pltpu.VMEM((4, 128, c), BF16),
        pltpu.VMEM((2, 64, h), BF16),
        pltpu.VMEM((2, 128, h), BF16),
        pltpu.VMEM((2, 2, 32, h), BF16),
        pltpu.VMEM((2, 4, 32, h), BF16),
        pltpu.VMEM((2, 2, 16, h), BF16),
        pltpu.VMEM((2, 2, 32, h), BF16),
    ]


class Gather:
    def __init__(self, links, full):
        k, h = links, full.shape[2] // 2
        a, b = pl.ds(0, h), pl.ds(h, h)
        x, y = k.x, k.y
        self.full, self.a, self.b = full, a, b
        self.a1 = RingGather(
            k, k.xs, k.xd, lambda j: full.at[y, rows_of(j * 32, 32), a], *split_rows(16)
        )
        self.b1 = RingGather(
            k, k.ys, k.yd, lambda j: full.at[j, rows_of(x * 32, 32), b], *split_rows(16)
        )
        self.a2 = RingGather(k, k.ys, k.yd, lambda j: full.at[j, :, a], *split_rows(64))
        self.b2 = RingGather(
            k, k.xs, k.xd, lambda j: full.at[:, rows_of(j * 32, 32), b], *split_rows(2)
        )
        self.k = k

    def put(self, start, value):
        self.full[self.k.y, rows_of(self.k.x * 32, 32), pl.ds(start, value.shape[1])] = value

    def s1(self):
        self.a1.start()
        self.b1.start()

    def s2(self):
        self.a1.middle()
        self.b1.middle()

    def s3(self):
        self.a1.finish()
        self.a2.start()
        self.b1.finish()
        self.b2.start()

    def s4(self):
        self.a2.middle()
        self.b2.middle()

    def fin(self):
        self.a2.finish()
        self.b2.finish()


def tiles(n, body):
    if n == 1:
        body(0)
    else:
        pl.loop(0, n)(body)


def cols(t):
    return pl.ds(pl.multiple_of(t * TILE, TILE), TILE)


def exchange(links, ring, devices, buf, value):
    me = ring[0]
    buf[me] = value
    return [links.send(buf.at[me], buf.at[me], devices[i]) for i in (1, 2, 3)]


def collect(copies, buf):
    for copy in copies:
        copy.wait_recv()
    return (buf[0] + buf[1]) + (buf[2] + buf[3])


def row_pack(first, second):
    width = first.shape[1]
    row = lax.broadcasted_iota(jnp.int32, (8, width), 0)
    one = jnp.where(row == 0, 1.0, 0.0).astype(BF16)
    two = jnp.where(row == 1, 1.0, 0.0).astype(BF16)

    def summed(pick, values):
        high = values.astype(BF16)
        rest = values - high.astype(F32)
        middle = rest.astype(BF16)
        low = (rest - middle.astype(F32)).astype(BF16)
        return mmt(pick, high) + (mmt(pick, middle) + mmt(pick, low))

    return summed(one, first) + summed(two, second)


def unpack_rows(packed):
    wide = jnp.concatenate([packed, jnp.zeros((120, packed.shape[1]), F32)], 0)
    return jnp.transpose(wide)


def scratch():
    s = {
        "send": pltpu.SemaphoreType.DMA((N_SEMS,)),
        "recv": pltpu.SemaphoreType.DMA((N_SEMS,)),
        "local": pltpu.SemaphoreType.DMA((16,)),
        "wqkv": pltpu.VMEM((BLK, 2304), BF16),
        "wup": pltpu.VMEM((BLK, 3072), BF16),
        "wout": pltpu.VMEM((768, BLK), BF16),
        "wdown": pltpu.VMEM((3072, BLK), BF16),
        "fg": pltpu.VMEM((4, TOK, ZC), BF16),
        "gg": pltpu.VMEM((4, TOK, ZC), BF16),
        "fw": pltpu.VMEM((TOK, BLK), BF16),
        "gw": pltpu.VMEM((TOK, BLK), BF16),
        "gwh": pltpu.VMEM((2, TOK, 192), BF16),
        "normed": pltpu.VMEM((TOK, BLK), BF16),
        "nT": pltpu.VMEM((BLK, TOK), BF16),
        "stx": pltpu.VMEM((4, 8, TOK), F32),
        "sty": pltpu.VMEM((4, 8, TOK), F32),
        "btx": pltpu.VMEM((4, 8, TOK), F32),
        "bty": pltpu.VMEM((4, 8, TOK), F32),
        "btz": pltpu.VMEM((4, 8, TOK), F32),
        "stat": pltpu.VMEM((TOK, 128), F32),
        "slope": pltpu.VMEM((OWN, 3072), F32),
        "joined": pltpu.VMEM((OWN, 2304), F32),
        "oacc": pltpu.VMEM((TOK, BLK), F32),
        "gacc": pltpu.VMEM((TOK, BLK), F32),
        "zp": pltpu.VMEM((2, 4, TOK, ZC), BF16),
        "zo": pltpu.VMEM((2, 2, 256, ZC), BF16),
        "zn": pltpu.VMEM((2, 2, TOK, ZC), BF16),
        "sdown": pltpu.VMEM((2, 3072, 192), BF16),
        "sattn": pltpu.VMEM((2, 768, 192), BF16),
        "sup": pltpu.VMEM((2, 192, 3072), BF16),
        "sqkv": pltpu.VMEM((2, 192, 2304), BF16),
    }
    for name, c in STREAMS:
        for i, item in enumerate(scatter_scratch(c)):
            s[name + str(i)] = item
    for name, c in GATHERS:
        s[name] = pltpu.VMEM((4, 128, c), BF16)
    return s


STREAMS = (
    ("Ba", 768),
    ("Bh1", 1536),
    ("Bh2", 1536),
    ("Fq", 2304),
    ("Fh1", 1536),
    ("Fh2", 1536),
    ("Dk", 1536),
)
GATHERS = (
    ("KV", 1536),
    ("H1", 1536),
    ("H2", 1536),
    ("G1", 1536),
    ("G2", 1536),
    ("AT", 768),
    ("GJ", 2304),
)


def kernel(names, feat, gout, w_qkv, w_up, w_out, w_down, *rest):
    layer_o, gin_o = rest[:2]
    (own_qkv, got_qkv, own_up, got_up, own_attn, got_attn, own_down, got_down) = rest[2:10]
    s = dict(zip(names, rest[10:]))
    k = Links(s["send"], s["recv"])
    z, core = k.z, k.core
    local = s["local"]
    fg, gg, fw, gw = s["fg"], s["gg"], s["fw"], s["gw"]

    loads = [
        pltpu.make_async_copy(src, dst, local.at[i])
        for i, (src, dst) in enumerate(
            (
                (gout, gg.at[z]),
                (feat, fg.at[z]),
                (w_out, s["wout"]),
                (w_down, s["wdown"]),
                (w_qkv, s["wqkv"]),
                (w_up, s["wup"]),
            )
        )
    ]
    for load in loads:
        load.start()
    k.barrier()

    def zgather(buf):
        return RingGather(k, k.zs, k.zd, lambda j: buf.at[j], *split_rows(256))

    def widen(buf, out):
        total = mm(buf[0], placed(ZC, BLK, 0))
        for j in (1, 2, 3):
            total += mm(buf[j], placed(ZC, BLK, j * ZC))
        out[...] = total.astype(BF16)

    zg, zf = zgather(gg), zgather(fg)
    loads[0].wait()
    zg.start()
    loads[1].wait()
    zf.start()
    zg.middle()
    zf.middle()
    zg.finish()
    widen(gg, gw)

    R = {}
    for name, c in STREAMS:
        part = s[name + "0"]
        R[name] = Scatter(k, part, [s[name + str(i)] for i in range(1, 7)])
    G = {name: Gather(k, s[name]) for name, c in GATHERS}

    def product(name, fn, n):
        part = s[name + "0"]

        def body(t):
            part[:, :, cols(t)] = fn(t).astype(BF16).reshape(4, 128, TILE)

        tiles(n, body)

    def back(base):
        return lambda t: mmt(
            gw[...], s["wdown"][pl.ds(pl.multiple_of(base + t * TILE, TILE), TILE), :]
        )

    def forth(name, base):
        return lambda t: mm(
            s["normed"][...], s[name][:, pl.ds(pl.multiple_of(base + t * TILE, TILE), TILE)]
        )

    loads[2].wait()
    product("Ba", lambda t: mmt(gw[...], s["wout"][...]), 1)
    R["Ba"].s1()
    loads[3].wait()
    product("Bh1", back(0), 2)
    R["Bh1"].s1()

    zf.finish()
    widen(fg, fw)
    wide = fw[...].astype(F32)
    ex = exchange(k, k.xs, k.xd, s["stx"], row_pack(wide, wide * wide))
    R["Ba"].s2()
    ey = exchange(k, k.ys, k.yd, s["sty"], collect(ex, s["stx"]))
    R["Bh1"].s2()
    stat = unpack_rows(collect(ey, s["sty"]))
    average = stat[:, 0:1] / D
    spread = stat[:, 1:2] / D - average * average
    inverse = lax.rsqrt(spread + EPS)
    lane = lax.broadcasted_iota(jnp.int32, (TOK, 128), 1)
    s["stat"][...] = jnp.where(lane == 0, average, inverse)
    s["normed"][...] = ((fw[...].astype(F32) - average) * inverse).astype(BF16)

    loads[4].wait()
    product("Fq", forth("wqkv", 0), 3)
    R["Fq"].s1()
    R["Ba"].s3()
    loads[5].wait()
    product("Fh1", forth("wup", 0), 2)
    R["Fh1"].s1()
    R["Bh1"].s3()
    R["Fq"].s2()
    R["Ba"].s4()
    product("Fh2", forth("wup", 1536), 2)
    R["Fh2"].s1()
    R["Fh1"].s2()
    R["Fq"].s3()
    R["Bh1"].s4()
    product("Bh2", back(1536), 2)
    R["Bh2"].s1()
    R["Fq"].s4()
    R["Fh2"].s2()
    R["Fh1"].s3()

    joined = s["joined"]
    low, high = R["Fq"].fin()
    joined[:, 0:1152] = low
    joined[:, 1152:2304] = high
    for h in range(HEADS):
        base = h * 3 * HS
        normal, _ = head_norm(joined[:, base + HS : base + 2 * HS])
        G["KV"].put(h * HS, normal.astype(BF16))
        G["KV"].put(768 + h * HS, joined[:, base + 2 * HS : base + 3 * HS].astype(BF16))
    G["KV"].s1()
    R["Fh1"].s4()
    R["Bh2"].s2()
    G["KV"].s2()
    R["Fh2"].s3()
    G["KV"].s3()

    slope = s["slope"]

    def activate(stream, gather, base):
        for i, value in enumerate(R[stream].fin()):
            G[gather].put(i * 768, gelu_value(value).astype(BF16))
            slope[:, base + i * 768 : base + (i + 1) * 768] = gelu_slope(value)

    def deactivate(stream, gather, base):
        for i, value in enumerate(R[stream].fin()):
            G[gather].put(
                i * 768, (value * slope[:, base + i * 768 : base + (i + 1) * 768]).astype(BF16)
            )

    activate("Fh1", "H1", 0)
    G["H1"].s1()
    R["Fh2"].s4()
    deactivate("Bh1", "G1", 0)
    G["G1"].s1()
    G["KV"].s4()
    R["Bh2"].s3()
    G["H1"].s2()
    G["G1"].s2()
    G["H1"].s3()
    s["nT"][...] = mmt(placed(BLK, BLK, 0), s["normed"][...]).astype(BF16)
    for c in range(2):
        s["gwh"][c] = (
            mm(gg[2 * c], placed(ZC, 192, 0)) + mm(gg[2 * c + 1], placed(ZC, 192, ZC))
        ).astype(BF16)

    G["KV"].fin()
    ba = R["Ba"].fin()
    kv = s["KV"]
    grads = s["joined"]
    dk0 = s["Dk0"]
    for h in range(HEADS):
        base = h * 3 * HS
        q_norm, q_inv = head_norm(joined[:, base : base + HS])
        q_b = q_norm.astype(BF16)
        keys = kv[:, :, h * HS : (h + 1) * HS].reshape(TOK, HS)
        values = kv[:, :, 768 + h * HS : 768 + (h + 1) * HS].reshape(TOK, HS)
        raised = jnp.exp(mmt(q_b, keys) * FACTOR)
        probs = raised / jnp.sum(raised, -1, keepdims=True)
        probs_b = probs.astype(BF16)
        G["AT"].put(h * HS, mm(probs_b, values).astype(BF16))
        part = ba[h // 3][:, (h % 3) * HS : (h % 3 + 1) * HS].astype(BF16)
        grad_probs = mmt(part, values)
        row_dot = jnp.sum(probs * grad_probs, -1, keepdims=True)
        grad_scores = (probs * (grad_probs - row_dot)).astype(BF16)
        grad_query = mm(grad_scores, keys) * FACTOR
        dk0[:, :, h * HS : (h + 1) * HS] = (
            (mtm(grad_scores, q_b) * FACTOR).astype(BF16).reshape(4, 128, HS)
        )
        dk0[:, :, 768 + h * HS : 768 + (h + 1) * HS] = (
            mtm(probs_b, part).astype(BF16).reshape(4, 128, HS)
        )
        grads[:, base : base + HS] = head_norm_back(grad_query, q_norm, q_inv)
    R["Dk"].s1()
    G["AT"].s1()
    activate("Fh2", "H2", 1536)
    G["H2"].s1()
    R["Bh2"].s4()
    R["Dk"].s2()
    G["AT"].s2()
    G["G1"].s3()
    G["H1"].s4()
    G["H2"].s2()
    R["Dk"].s3()
    deactivate("Bh2", "G2", 1536)
    G["G2"].s1()
    G["AT"].s3()
    G["G1"].s4()
    R["Dk"].s4()
    G["H2"].s3()
    G["G2"].s2()
    G["AT"].s4()

    key_grad, value_grad = R["Dk"].fin()
    for h in range(HEADS):
        base = h * 3 * HS
        k_norm, k_inv = head_norm(joined[:, base + HS : base + 2 * HS])
        G["GJ"].put(base, grads[:, base : base + HS].astype(BF16))
        G["GJ"].put(
            base + HS,
            head_norm_back(key_grad[:, h * HS : (h + 1) * HS], k_norm, k_inv).astype(BF16),
        )
        G["GJ"].put(base + 2 * HS, value_grad[:, h * HS : (h + 1) * HS].astype(BF16))
    G["GJ"].s1()
    G["G2"].s3()

    oacc, gacc = s["oacc"], s["gacc"]

    def rows_tile(name, t):
        return s[name][:, :, cols(t)].reshape(TOK, TILE)

    copies = []
    shares = []

    def share(stage, own_out, got_out, index, slot):
        mine = pltpu.make_async_copy(stage.at[core, *index], own_out.at[index], local.at[slot])
        mine.start()
        copies.append(mine)
        shares.append(k.send(stage.at[1 - core, *index], got_out.at[index], k.cd))

    def use_hidden(name, weight, stage, base, n, first):
        if first:
            oacc[...] = jnp.zeros_like(oacc)

        def body(t):
            block = rows_tile(name, t)
            at = pl.ds(pl.multiple_of(base + t * TILE, TILE), TILE)
            oacc[...] += mm(block, s[weight][at, :])
            for c in range(2):
                s[stage][c, at, :] = mtm(block, s["gwh"][c]).astype(BF16)

        tiles(n, body)

    def use_grads(name, weight, stage, base, n, first):
        if first:
            gacc[...] = jnp.zeros_like(gacc)

        def body(t):
            block = rows_tile(name, t)
            at = pl.ds(pl.multiple_of(base + t * TILE, TILE), TILE)
            gacc[...] += mmt(block, s[weight][:, at])
            both = mm(s["nT"][...], block).astype(BF16)
            s[stage][0, :, at] = both[0:192]
            s[stage][1, :, at] = both[192:384]

        tiles(n, body)

    G["H1"].fin()
    use_hidden("H1", "wdown", "sdown", 0, 2, True)
    share(s["sdown"], own_down, got_down, (pl.ds(0, 1536), slice(None)), 6)
    G["GJ"].s2()
    G["H2"].s4()
    G["G1"].fin()
    use_grads("G1", "wup", "sup", 0, 2, True)
    share(s["sup"], own_up, got_up, (slice(None), pl.ds(0, 1536)), 7)
    G["G2"].s4()
    G["GJ"].s3()
    G["AT"].fin()
    use_hidden("AT", "wout", "sattn", 0, 1, False)
    share(s["sattn"], own_attn, got_attn, (slice(None), slice(None)), 8)
    G["H2"].fin()
    use_hidden("H2", "wdown", "sdown", 1536, 2, False)
    share(s["sdown"], own_down, got_down, (pl.ds(1536, 1536), slice(None)), 9)

    def zscatter(i, total):
        part = s["zp"].at[i]
        rounded = total.astype(BF16)
        for j in range(4):
            row = lax.broadcasted_iota(jnp.int32, (BLK, ZC), 0)
            column = lax.broadcasted_iota(jnp.int32, (BLK, ZC), 1)
            pick = jnp.where(row == column + j * ZC, 1.0, 0.0).astype(BF16)
            part[j] = mm(rounded, pick).astype(BF16)
        return RingSum(
            k, k.zs, k.zd, lambda j: part.at[j], *split_rows(256), s["zo"].at[i], s["zn"].at[i]
        )

    zl = zscatter(0, oacc[...])
    zl.start()
    G["GJ"].s4()
    G["G2"].fin()
    use_grads("G2", "wup", "sup", 1536, 2, False)
    share(s["sup"], own_up, got_up, (slice(None), pl.ds(1536, 1536)), 10)
    zl.middle()
    layer_o[...] = (fg[z].astype(F32) + zl.total()).astype(BF16)

    G["GJ"].fin()
    use_grads("GJ", "wqkv", "sqkv", 0, 3, False)
    total = gacc[...]
    average, inverse = s["stat"][:, 0:1], s["stat"][:, 1:2]
    normal = (fw[...].astype(F32) - average) * inverse
    zi = zscatter(1, total)
    zi.start()
    ez = exchange(k, k.zs, k.zd, s["btz"], row_pack(total, total * normal))
    share(s["sqkv"], own_qkv, got_qkv, (slice(None), slice(None)), 11)
    zi.middle()
    ex = exchange(k, k.xs, k.xd, s["btx"], collect(ez, s["btz"]))
    ey = exchange(k, k.ys, k.yd, s["bty"], collect(ex, s["btx"]))
    summed = zi.total()
    sums = unpack_rows(collect(ey, s["bty"]))
    normal_own = (fg[z].astype(F32) - average) * inverse
    correction = summed - sums[:, 0:1] / D - normal_own * (sums[:, 1:2] / D)
    gin_o[...] = (gg[z].astype(F32) + inverse * correction).astype(BF16)

    for copy in copies:
        copy.wait()
    for copy in shares:
        copy.wait_recv()
    for copy in k.started:
        copy.wait_send()


def on_device(features, w_qkv, w_up, w_out, w_down, grad_out):
    qkv_flat = w_qkv.reshape(BLK, 2304)
    out_flat = w_out.reshape(768, BLK)
    shapes = scratch()
    any_spec = pl.BlockSpec(memory_space=pl.ANY)
    vmem_spec = pl.BlockSpec(memory_space=pltpu.VMEM)

    def pair(*shape):
        return [jax.ShapeDtypeStruct(shape, BF16)] * 2

    names = tuple(shapes)
    outs = pl.pallas_call(
        lambda *refs: kernel(names, *refs),
        out_shape=[jax.ShapeDtypeStruct((TOK, ZC), BF16)] * 2
        + pair(192, 2304)
        + pair(192, 3072)
        + pair(768, 192)
        + pair(3072, 192),
        in_specs=[any_spec] * 6,
        out_specs=[vmem_spec] * 2 + [any_spec] * 8,
        scratch_shapes=list(shapes.values()),
        compiler_params=pltpu.CompilerParams(
            collective_id=0, has_side_effects=True, vmem_limit_bytes=60 * 1024 * 1024
        ),
        cost_estimate=pl.CostEstimate(
            flops=11_000_000_000, bytes_accessed=20_000_000, transcendentals=1_000_000
        ),
    )(features, grad_out, qkv_flat, w_up, out_flat, w_down)
    layer_out, grad_in = outs[:2]

    def both(i):
        return outs[i].astype(F32) + outs[i + 1].astype(F32)

    return (
        layer_out,
        grad_in,
        both(2).reshape(192, HEADS, 3 * HS),
        both(4),
        both(6).reshape(HEADS, HS, 192),
        both(8),
    )


def solution(mesh):
    in_specs = (
        P("dp", ("mx", "my")),
        P("mx", "my", None),
        P("mx", "my"),
        P("my", None, "mx"),
        P("my", "mx"),
        P("dp", ("mx", "my")),
    )
    out_specs = (
        P("dp", ("mx", "my")),
        P("dp", ("mx", "my")),
        P(("mx", "dp"), "my", None),
        P(("mx", "dp"), "my"),
        P("my", None, ("mx", "dp")),
        P("my", ("mx", "dp")),
    )
    return jax.shard_map(
        on_device, mesh=mesh, in_specs=in_specs, out_specs=out_specs, check_vma=False
    )
```

time: 797 us -> 187 us (0.23)
  waiting for transfers between devices: 363 us -> 0 us
  blocking collectives: 322 us -> 0 us
  Pallas kernels: 0 us -> 164 us
  matrix products: 56.8 us -> 0 us
  other arithmetic: 25 us -> 3.44 us
  between operations: 14.2 us -> 0.71 us
    reduce_scatter x10 -> x0, waiting for transfers between devices: 258 us -> none  [the longest x1 75.4 us: on_device(): lax.psum_scatter(value_part, 'mx', scatter_dimension=0, tiled=True)]
    psum x2 -> x0, blocking collectives: 217 us -> none  [the longest x1 177 us: on_device(): lax.psum((jnp.sum(grad_normed, 1), jnp.sum(grad_normed * normal_own, 1)),...]
    pallas_call x0 -> x1, Pallas kernels: none -> 164 us  [on_device(): pl.pallas_call(lambda *refs: kernel(names, *refs), out_shape=[jax.ShapeDt...]
    all_gather x5 -> x0, blocking collectives: 104 us -> none  [the longest x1 26.7 us: on_device(): lax.all_gather(key_b, 'mx', axis=0, tiled=True)]
    all_gather x3 -> x0, waiting for transfers between devices: 104 us -> none  [the longest x1 45.5 us: on_device(): lax.all_gather(grad_hidden_b, 'mx', axis=0, tiled=True)]
    dot_general x17 -> x0, matrix products: 54.4 us -> none  [the longest x4 17 us: contract_first(): lax.dot_general(left_side, right_side, (((0,), (0,)), ((), ())), preferre...]
    concatenate x2 -> x0, other arithmetic: 12.8 us -> none  [the longest x1 9.03 us: on_device(): jnp.concatenate([jnp.dot(part_rows, qkv_flat, preferred_element_type=jnp....]
  transfers between devices with their start and end apart: 13 -> 0, of which waited for: 8 -> 0; matrix products, arithmetic and copies ran while one was open for 7% -> 0% of each run, Pallas kernels for 0% -> 0%
where the time goes in v1:
time: 187 us
  Pallas kernels  164 us (88%)
  local copies, waits for them, and re-layouts  18.3 us (10%)
  other arithmetic  3.44 us (2%)
    pallas_call x1, Pallas kernels, on_device(): pl.pallas_call(lambda *refs: kernel(names, *refs), out_shape=[jax.ShapeDt...  164 us
    unnamed x19, local copies, waits for them, and re-layouts  14.7 us

profile of v1, /device:TPU:0, one launch (start us, length us, event | category | flops | bytes accessed | tf_op | source)
XLA Modules:
  0.0 186.6 jit_solution(6000071345845501178)
XLA Ops:
  0.6 1.7 copy.21.refs_0_
  2.3 1.7 copy.22.refs_1_
  3.9 2.8 %copy.20 = bf16[384,6,384]{0,2,1:T(8,128)(2,1)S(1)} copy(bf16[384,6,384]{2,0,1:T(8,128)(2,1)} %param.7) | data formatting | bytes 3538944 | tf_op args[1]
  6.7 2.3 %copy.23.refs_2_ = bf16[384,2304]{1,0:T(8,128)(2,1)} copy(bf16[384,2304]{0,1:T(8,128)(2,1)S(1)} %bitcast.8) | data formatting | bytes 3538944 | tf_op jit(solution)/shard_map/reshape | solution.py:710
  9.0 164.1 %shard_map.109 = (bf16[512,96]{1,0:T(8,128)(2,1)}, bf16[512,96]{1,0:T(8,128)(2,1)}, bf16[192,2304]{1,0:T(8,128)(2,1)}, bf16[192,2304]{1,0:T(8,128)(2,1)}, bf16[1...) custom-call(bf16[512,96]{1,0:T(8,128)(2,1)} %copy.21.refs_0_, ...), custom_call_target="tpu_custom_call" | custom-call | flops 11000000512 | bytes 20000000 | tf_op jit(solution)/shard_map/pallas_call | solution.py:720
  173.2 0.0 copy-start.4
  173.2 0.0 copy-start.5
  173.2 1.8 copy.24
  175.0 1.6 copy.25
  176.6 1.2 convert_add_fusion.3
  177.8 1.1 copy.27
  178.9 0.0 copy-done.4
  178.9 0.0 copy-done.5
  178.9 0.2 convert_add_fusion.2
  179.1 0.0 copy-start.2
  179.1 0.0 copy-start.3
  179.1 1.3 copy.31
  180.4 0.4 copy-done.2
  180.9 0.5 copy-done.3
  181.4 1.7 convert_add_fusion.1
  183.1 0.0 copy-done
  183.1 1.0 copy-done.1
  184.1 0.3 convert_add_fusion
  184.4 2.2 %copy.28 = f32[3072,192]{0,1:T(8,128)} copy(f32[3072,192]{1,0:T(8,128)S(1)} %convert_add_fusion) | data formatting | bytes 4718592
  (2 shorter events, 0.0 us)
Async XLA Ops:
  173.2 5.7 %copy-start.4 = (bf16[192,2304]{1,0:T(8,128)(2,1)S(1)}, bf16[192,2304]{1,0:T(8,128)(2,1)}, u32[]{:S(2)}) copy-start(bf16[192,2304]{1,0:T(8,128)(2,1)} %get-tuple-element.18) | copy-start | bytes 2654212
  173.2 5.7 %copy-start.5 = (bf16[192,2304]{1,0:T(8,128)(2,1)S(1)}, bf16[192,2304]{1,0:T(8,128)(2,1)}, u32[]{:S(2)}) copy-start(bf16[192,2304]{1,0:T(8,128)(2,1)} %get-tuple-element.19) | copy-start | bytes 2654212
  179.1 1.8 copy-start.2
  179.1 2.3 %copy-start.3 = (bf16[192,3072]{1,0:T(8,128)(2,1)S(1)}, bf16[192,3072]{1,0:T(8,128)(2,1)}, u32[]{:S(2)}) copy-start(bf16[192,3072]{1,0:T(8,128)(2,1)} %get-tuple-element.21) | copy-start | bytes 3538948
  181.4 1.7 copy-start
  181.4 2.7 %copy-start.1 = (bf16[3072,192]{1,0:T(8,128)(2,1)S(1)}, bf16[3072,192]{1,0:T(8,128)(2,1)}, u32[]{:S(2)}) copy-start(bf16[3072,192]{1,0:T(8,128)(2,1)} %get-tuple-element.25) | copy-start | bytes 3538948

commit v2 on v1

v2 whole, which is shorter than its diff:
```python
import math

import jax
import jax.numpy as jnp
from jax import lax
from jax.experimental import pallas as pl
from jax.experimental.pallas import tpu as pltpu
from jax.sharding import PartitionSpec as P

D = 6144
EPS = 1e-06
F32 = jnp.float32
BF16 = jnp.bfloat16
MESH = pl.DeviceIdType.MESH
HEADS = 6
HS = 128
TOK = 512
OWN = 32
BLK = 384
ZC = 96
FACTOR = 1.0 / math.sqrt(HS)
N_SEMS = 340
TILE = 768
SETTLE = 16


def mm(a, b):
    return lax.dot_general(a, b, (((1,), (0,)), ((), ())), preferred_element_type=F32)


def mmt(a, b):
    return lax.dot_general(a, b, (((1,), (1,)), ((), ())), preferred_element_type=F32)


def mtm(a, b):
    return lax.dot_general(a, b, (((0,), (0,)), ((), ())), preferred_element_type=F32)


def gelu_value(values):
    return 0.5 * values * (1.0 + lax.erf(values / math.sqrt(2.0)))


def gelu_slope(values):
    return 0.5 * (1.0 + lax.erf(values / math.sqrt(2.0))) + values * jnp.exp(
        -0.5 * values * values
    ) / math.sqrt(2.0 * math.pi)


def head_norm(values):
    average = jnp.mean(values, -1, keepdims=True)
    spread = jnp.mean(values * values, -1, keepdims=True) - average * average
    inverse = lax.rsqrt(spread + EPS)
    return ((values - average) * inverse, inverse)


def head_norm_back(gradient, normal, inverse):
    first_mean = jnp.mean(gradient, -1, keepdims=True)
    second_mean = jnp.mean(gradient * normal, -1, keepdims=True)
    return inverse * (gradient - first_mean - normal * second_mean)


def identity(n):
    row = lax.broadcasted_iota(jnp.int32, (n, n), 0)
    column = lax.broadcasted_iota(jnp.int32, (n, n), 1)
    return jnp.where(row == column, 1.0, 0.0).astype(BF16)


def add_to(ref, more):
    ref[...] = (ref[...].astype(F32) + more[...].astype(F32)).astype(ref.dtype)


class Links:
    def __init__(self, send, recv):
        self.send_sems, self.recv_sems, self.count, self.started = send, recv, 0, []
        self.turn = 0
        mx = lax.axis_index("mx")
        self.x, self.y = lax.rem(mx, 4), lax.div(mx, 4)
        self.z, self.core = lax.axis_index("my"), lax.axis_index("dp")
        x, y, z = self.x, self.y, self.z
        self.xs = [lax.rem(x + i, 4) for i in range(4)]
        self.ys = [lax.rem(y + i, 4) for i in range(4)]
        self.zs = [lax.rem(z + i, 4) for i in range(4)]
        self.xd = [{"mx": y * 4 + v} for v in self.xs]
        self.yd = [{"mx": v * 4 + x} for v in self.ys]
        self.zd = [{"my": v} for v in self.zs]
        self.cd = {"dp": 1 - self.core}

    def send(self, src, dst, device):
        i = self.count
        self.count += 1
        copy = pltpu.make_async_remote_copy(
            src_ref=src,
            dst_ref=dst,
            send_sem=self.send_sems.at[i],
            recv_sem=self.recv_sems.at[i],
            device_id=device,
            device_id_type=MESH,
        )
        copy.start()
        self.started.append((self.turn, copy))
        return copy

    def settle(self, turn):
        self.turn = turn + 1
        while self.started and self.started[0][0] <= turn - SETTLE:
            self.started.pop(0)[1].wait_send()

    def barrier(self):
        sem = pltpu.get_barrier_semaphore()
        peers = self.xd[1:] + self.yd[1:] + self.zd[1:] + [self.cd]
        for peer in peers:
            pl.semaphore_signal(sem, inc=1, device_id=peer, device_id_type=MESH)
        pl.semaphore_wait(sem, len(peers))


def rows_of(start, size):
    return pl.ds(pl.multiple_of(start, 16), size)


class RingSum:
    def __init__(self, links, ring, devices, chunk, first, second, opp, near):
        self.k, self.ring, self.dev = links, ring, devices
        self.chunk, self.first, self.second, self.opp, self.near = chunk, first, second, opp, near

    def start(self):
        far, left, right = (self.chunk(self.ring[i]) for i in (2, 3, 1))
        to_left, to_right = self.near.at[1], self.near.at[0]
        self.far_left = self.k.send(self.first(far), self.opp.at[1], self.dev[3])
        self.far_right = self.k.send(self.second(far), self.opp.at[0], self.dev[1])
        self.near_copies = [
            self.k.send(self.second(left), self.second(to_left), self.dev[3]),
            self.k.send(self.first(right), self.first(to_right), self.dev[1]),
        ]

    def middle(self):
        left, right = self.chunk(self.ring[3]), self.chunk(self.ring[1])
        self.far_left.wait_recv()
        part = self.first(left)
        add_to(part, self.opp.at[1])
        self.near_copies.append(self.k.send(part, self.first(self.near.at[1]), self.dev[3]))
        self.far_right.wait_recv()
        part = self.second(right)
        add_to(part, self.opp.at[0])
        self.near_copies.append(self.k.send(part, self.second(self.near.at[0]), self.dev[1]))

    def total(self):
        for copy in self.near_copies:
            copy.wait_recv()
        own = self.chunk(self.ring[0])
        return own[...].astype(F32) + self.near[0].astype(F32) + self.near[1].astype(F32)


class RingGather:
    def __init__(self, links, ring, devices, chunk, first, second):
        self.k, self.ring, self.dev = links, ring, devices
        self.chunk, self.first, self.second = chunk, first, second

    def start(self):
        own = self.chunk(self.ring[0])
        self.to_left = self.k.send(own, own, self.dev[3])
        self.to_right = self.k.send(own, own, self.dev[1])

    def middle(self):
        self.to_right.wait_recv()
        part = self.first(self.chunk(self.ring[3]))
        self.on_right = self.k.send(part, part, self.dev[1])
        self.to_left.wait_recv()
        part = self.second(self.chunk(self.ring[1]))
        self.on_left = self.k.send(part, part, self.dev[3])

    def finish(self):
        self.on_right.wait_recv()
        self.on_left.wait_recv()


def split_rows(n):
    return (lambda r: r.at[pl.ds(0, n)]), (lambda r: r.at[pl.ds(n, n)])


class Scatter:
    def __init__(self, links, part, bufs, ca, cb, w):
        k = links
        a, b = pl.ds(0, ca), pl.ds(ca, cb)
        a1o, a1n, b1o, b1n, a2, b2, a2o, a2n, b2o, b2n = bufs
        self.mid_a, self.mid_b = a2, b2
        if w:
            a2_chunk, a2_split = (lambda j: a2.at[:, part_of(j, w)]), split_rows(64)
            b2_chunk, b2_split = (
                lambda j: b2.at[pl.ds(lax.rem(j, 2) * 2, 2), :, part_of(lax.div(j, 2), w)]
            ), split_rows(1)
        else:
            a2_chunk, a2_split = (lambda j: a2.at[rows_of(j * 32, 32), :]), split_rows(16)
            b2_chunk, b2_split = (lambda j: b2.at[j]), split_rows(16)
        self.a1 = RingSum(k, k.ys, k.yd, lambda j: part.at[j, :, a], *split_rows(64), a1o, a1n)
        self.b1 = RingSum(
            k, k.xs, k.xd, lambda j: part.at[:, rows_of(j * 32, 32), b], *split_rows(2), b1o, b1n
        )
        self.a2 = RingSum(k, k.xs, k.xd, a2_chunk, *a2_split, a2o, a2n)
        self.b2 = RingSum(k, k.ys, k.yd, b2_chunk, *b2_split, b2o, b2n)

    def s1(self):
        self.a1.start()
        self.b1.start()

    def s2(self):
        self.a1.middle()
        self.b1.middle()

    def s3(self):
        self.mid_a[...] = self.a1.total().astype(self.mid_a.dtype)
        self.a2.start()
        self.mid_b[...] = self.b1.total().astype(self.mid_b.dtype)
        self.b2.start()

    def s4(self):
        self.a2.middle()
        self.b2.middle()

    def fin(self):
        return self.a2.total(), self.b2.total()


def part_of(j, w):
    return pl.ds(pl.multiple_of(j * w, 128), w)


def scatter_scratch(ca, cb, w, kind):
    found = [
        pltpu.VMEM((4, 128, ca + cb), BF16),
        pltpu.VMEM((2, 64, ca), BF16),
        pltpu.VMEM((2, 128, ca), BF16),
        pltpu.VMEM((2, 2, 32, cb), BF16),
        pltpu.VMEM((2, 4, 32, cb), BF16),
        pltpu.VMEM((128, ca), kind),
        pltpu.VMEM((4, 32, cb), kind),
    ]
    if w:
        return found + [
            pltpu.VMEM((2, 64, w), kind),
            pltpu.VMEM((2, 128, w), kind),
            pltpu.VMEM((2, 1, 32, w), kind),
            pltpu.VMEM((2, 2, 32, w), kind),
        ]
    return found + [
        pltpu.VMEM((2, 16, ca), kind),
        pltpu.VMEM((2, 32, ca), kind),
        pltpu.VMEM((2, 16, cb), kind),
        pltpu.VMEM((2, 32, cb), kind),
    ]


class Gather:
    def __init__(self, links, full, ca, cb, w):
        k = links
        a, b = pl.ds(0, ca), pl.ds(ca, cb)
        x, y = k.x, k.y
        self.full, self.ca, self.w, self.k = full, ca, w, k
        if w:
            a1_chunk, a1_split = (lambda j: full.at[y, :, part_of(j, w)]), split_rows(64)
            b1_chunk, b1_split = (
                lambda j: full.at[
                    pl.ds(lax.rem(j, 2) * 2, 2),
                    rows_of(x * 32, 32),
                    part_of(4 + lax.div(j, 2), w),
                ]
            ), split_rows(1)
        else:
            a1_chunk, a1_split = (lambda j: full.at[y, rows_of(j * 32, 32), a]), split_rows(16)
            b1_chunk, b1_split = (lambda j: full.at[j, rows_of(x * 32, 32), b]), split_rows(16)
        self.a1 = RingGather(k, k.xs, k.xd, a1_chunk, *a1_split)
        self.b1 = RingGather(k, k.ys, k.yd, b1_chunk, *b1_split)
        self.a2 = RingGather(k, k.ys, k.yd, lambda j: full.at[j, :, a], *split_rows(64))
        self.b2 = RingGather(
            k, k.xs, k.xd, lambda j: full.at[:, rows_of(j * 32, 32), b], *split_rows(2)
        )

    def put(self, i, value):
        at = pl.ds(0, self.ca) if i == 0 else pl.ds(self.ca, value.shape[1])
        self.full[self.k.y, rows_of(self.k.x * 32, 32), at] = value

    def put_head(self, i, start, value):
        x, y, n = self.k.x, self.k.y, value.shape[1]
        if i == 0:
            self.full[y, :, pl.ds(pl.multiple_of(x * self.w + start, 128), n)] = value
        else:
            at = pl.ds(pl.multiple_of((4 + lax.div(y, 2)) * self.w + start, 128), n)
            half = pl.ds(lax.rem(y, 2) * 2, 2)
            self.full[half, rows_of(x * 32, 32), at] = value.reshape(2, 32, n)

    def s1(self):
        self.a1.start()
        self.b1.start()

    def s2(self):
        self.a1.middle()
        self.b1.middle()

    def s3(self):
        self.a1.finish()
        self.a2.start()
        self.b1.finish()
        self.b2.start()

    def s4(self):
        self.a2.middle()
        self.b2.middle()

    def fin(self):
        self.a2.finish()
        self.b2.finish()


class KeyValue:
    def __init__(self, links, s):
        k = links
        x, y = k.x, k.y
        self.k = k
        a, b, da, db = s["KVa"], s["KVb"], s["DKa"], s["DKb"]
        self.a, self.b, self.da, self.db, self.mid, self.got = a, b, da, db, s["DKm"], s["DKg"]
        self.mine = pl.ds(lax.rem(y, 2) * 2, 2)
        self.other = pl.ds(2 - lax.rem(y, 2) * 2, 2)
        self.mate = {"mx": (y + 1 - 2 * lax.rem(y, 2)) * 4 + x}
        self.ga = RingGather(k, k.ys, k.yd, lambda j: a.at[j], *split_rows(64))
        self.gb = RingGather(k, k.xs, k.xd, lambda j: b.at[j], *split_rows(2))
        self.ra = RingSum(
            k, k.ys, k.yd, lambda j: da.at[j], *split_rows(64), s["DKao"], s["DKan"]
        )
        self.rb = RingSum(k, k.xs, k.xd, lambda j: db.at[j], *split_rows(2), s["DKbo"], s["DKbn"])

    def s1(self):
        own = self.b.at[self.k.x, self.mine]
        self.pair = self.k.send(own, own, self.mate)
        self.ga.start()

    def s2(self):
        self.pair.wait_recv()
        self.gb.start()
        self.ga.middle()

    def s3(self):
        self.gb.middle()

    def fin(self):
        self.ga.finish()
        self.gb.finish()

    def d1(self):
        self.rb.start()
        self.ra.start()

    def d2(self):
        self.rb.middle()
        self.ra.middle()

    def d3(self):
        self.mid[...] = self.rb.total()
        self.back = self.k.send(self.mid.at[self.other], self.got, self.mate)
        return self.ra.total()

    def d4(self):
        self.back.wait_recv()
        return self.mid[self.mine] + self.got[...]


def tiles(n, body):
    if n == 1:
        body(0)
    else:
        pl.loop(0, n)(body)


def cols(t):
    return pl.ds(pl.multiple_of(t * TILE, TILE), TILE)


def exchange(links, ring, devices, buf, value):
    me = ring[0]
    buf[me] = value
    return [links.send(buf.at[me], buf.at[me], devices[i]) for i in (1, 2, 3)]


def collect(copies, buf):
    for copy in copies:
        copy.wait_recv()
    return (buf[0] + buf[1]) + (buf[2] + buf[3])


def row_pack(first, second):
    row = lax.broadcasted_iota(jnp.int32, (2, TOK), 0)
    return jnp.where(row == 0, first, second)


STREAMS = (
    ("Ba", 512, 256, HS, F32),
    ("Bh1", 640, 896, 0, BF16),
    ("Bh2", 640, 896, 0, BF16),
    ("Fq", 1536, 768, 3 * HS, F32),
    ("Fh1", 640, 896, 0, BF16),
    ("Fh2", 640, 896, 0, BF16),
)
GATHERS = (
    ("H1", 640, 896, 0),
    ("H2", 640, 896, 0),
    ("G1", 640, 896, 0),
    ("G2", 640, 896, 0),
    ("AT", 512, 256, HS),
    ("GJ", 1536, 768, 3 * HS),
)


ORDER = (
    "enter",
    "zf start",
    "zg mid",
    "zf mid",
    "zg_end",
    "load 3",
    "M Bh1",
    "Bh1 s1",
    "zf_end",
    "M Bh2",
    "Bh2 s1",
    "clear",
    "load 2",
    "M Ba",
    "Bh1 s2",
    "Ba s1",
    "stat_y",
    "Bh2 s2",
    "norm",
    "load 4",
    "M Fq",
    "Fq s1",
    "load 5",
    "M Fh1",
    "M Fh2",
    "Bh2 s3",
    "Fh1 s1",
    "Bh1 s3",
    "Fq s2",
    "Fh2 s1",
    "Ba s2",
    "Bh2 s4",
    "Fh1 s2",
    "Bh1 s4",
    "Fq s3",
    "Fh2 s2",
    "Ba s3",
    "Fh1 s3",
    "Fq s4",
    "Fh2 s3",
    "Fh1 s4",
    "Ba s4",
    "project",
    "KV s1",
    "act Fh1",
    "H1 s1",
    "deact Bh1",
    "KV s2",
    "Fh2 s4",
    "G1 s1",
    "H1 s2",
    "KV s3",
    "act Fh2",
    "H1 s3",
    "KV fin",
    "attend",
    "KV d1",
    "G1 s2",
    "deact Bh2",
    "AT s1",
    "G2 s1",
    "H1 s4",
    "KV d2",
    "H2 s1",
    "G1 s3",
    "AT s2",
    "G2 s2",
    "H1 fin",
    "acc H1",
    "dw H1",
    "KV d3",
    "H2 s2",
    "KV d4",
    "GJ s1",
    "G1 s4",
    "G2 s3",
    "H2 s3",
    "AT s3",
    "GJ s2",
    "G1 fin",
    "dw G1",
    "acc G1",
    "G2 s4",
    "H2 s4",
    "AT s4",
    "GJ s3",
    "G2 fin",
    "acc G2",
    "dw G2",
    "H2 fin",
    "acc H2",
    "AT fin",
    "dw AT",
    "acc AT",
    "zl_start",
    "dw H2",
    "GJ s4",
    "zl_mid",
    "layer_out",
    "GJ fin",
    "acc GJ",
    "gin",
    "dw GJ",
    "zi_mid",
    "back_x",
    "back_y",
    "gin_out",
)


def scratch():
    s = {
        "send": pltpu.SemaphoreType.DMA((N_SEMS,)),
        "recv": pltpu.SemaphoreType.DMA((N_SEMS,)),
        "local": pltpu.SemaphoreType.DMA((16,)),
        "wqkv": pltpu.VMEM((HEADS, BLK, 3 * HS), BF16),
        "wup": pltpu.VMEM((BLK, 3072), BF16),
        "wout": pltpu.VMEM((768, BLK), BF16),
        "wdown": pltpu.VMEM((3072, BLK), BF16),
        "fg": pltpu.VMEM((4, ZC, TOK), BF16),
        "gg": pltpu.VMEM((4, ZC, TOK), BF16),
        "gw": pltpu.VMEM((TOK, BLK), BF16),
        "normed": pltpu.VMEM((TOK, BLK), BF16),
        "nT": pltpu.VMEM((BLK, TOK), BF16),
        "stx": pltpu.VMEM((4, 2, TOK), F32),
        "sty": pltpu.VMEM((4, 2, TOK), F32),
        "btx": pltpu.VMEM((4, 2, TOK), F32),
        "bty": pltpu.VMEM((4, 2, TOK), F32),
        "btz": pltpu.VMEM((4, 2, TOK), F32),
        "stat": pltpu.VMEM((2, TOK), F32),
        "slope": pltpu.VMEM((OWN, 3072), F32),
        "oacc": pltpu.VMEM((TOK, BLK), F32),
        "gacc": pltpu.VMEM((TOK, BLK), F32),
        "zp": pltpu.VMEM((2, 4, ZC, TOK), BF16),
        "zo": pltpu.VMEM((2, 2, 48, TOK), BF16),
        "zn": pltpu.VMEM((2, 2, ZC, TOK), BF16),
        "sdown": pltpu.VMEM((2, 192, 3072), BF16),
        "sattn": pltpu.VMEM((2, HEADS, 192, HS), BF16),
        "sup": pltpu.VMEM((2, 192, 3072), BF16),
        "sqkv": pltpu.VMEM((2, HEADS, 192, 3 * HS), BF16),
    }
    for name, ca, cb, w, kind in STREAMS:
        for i, item in enumerate(scatter_scratch(ca, cb, w, kind)):
            s[name + str(i)] = item
    for name, ca, cb, w in GATHERS:
        s[name] = pltpu.VMEM((4, 128, ca + cb), BF16)
    for name, shape, kind in (
        ("KVa", (4, 128, 256), BF16),
        ("KVb", (4, 4, 32, 256), BF16),
        ("DKa", (4, 128, 256), BF16),
        ("DKb", (4, 4, 32, 256), BF16),
        ("DKao", (2, 64, 256), BF16),
        ("DKan", (2, 128, 256), BF16),
        ("DKbo", (2, 2, 32, 256), BF16),
        ("DKbn", (2, 4, 32, 256), BF16),
        ("DKm", (4, 32, 256), F32),
        ("DKg", (2, 32, 256), F32),
        ("ja", (128, 3 * HS), F32),
        ("jb", (64, 3 * HS), F32),
    ):
        s[name] = pltpu.VMEM(shape, kind)
    return s


def kernel(names, feat, gout, w_qkv, w_up, w_out, w_down, *rest):
    layer_o, gin_o = rest[:2]
    (own_qkv, got_qkv, own_up, got_up, own_attn, got_attn, own_down, got_down) = rest[2:10]
    s = dict(zip(names, rest[10:]))
    k = Links(s["send"], s["recv"])
    z, core = k.z, k.core
    local = s["local"]
    fg, gg, gw = s["fg"], s["gg"], s["gw"]

    loads = [
        pltpu.make_async_copy(src, dst, local.at[i])
        for i, (src, dst) in enumerate(
            (
                (gout, gg.at[z]),
                (feat, fg.at[z]),
                (w_out, s["wout"]),
                (w_down, s["wdown"]),
                (w_qkv, s["wqkv"]),
                (w_up, s["wup"]),
            )
        )
    ]
    for load in loads:
        load.start()
    k.barrier()

    def wide(buf):
        return buf[...].reshape(BLK, TOK)

    def ring_z(buf):
        return RingGather(k, k.zs, k.zd, lambda j: buf.at[j], *split_rows(48))

    R = {}
    for name, ca, cb, w, _ in STREAMS:
        bufs = [s[name + str(i)] for i in range(1, 11)]
        R[name] = Scatter(k, s[name + "0"], bufs, ca, cb, w)
    G = {name: Gather(k, s[name], ca, cb, w) for name, ca, cb, w in GATHERS}
    KV = KeyValue(k, s)
    ops = {}
    held = {}
    for table in (R, G):
        for name, stream in table.items():
            for step in ("s1", "s2", "s3", "s4", "fin"):
                ops[name + " " + step] = getattr(stream, step)
    for step in ("s1", "s2", "s3", "fin", "d1", "d2"):
        ops["KV " + step] = getattr(KV, step)
    every = slice(None)
    oacc, gacc, slope = s["oacc"], s["gacc"], s["slope"]
    zf, zg = ring_z(fg), ring_z(gg)

    def op(function):
        ops[function.__name__] = function
        return function

    @op
    def enter():
        loads[0].wait()
        zg.start()
        loads[1].wait()

    ops["zf start"] = zf.start
    ops["zg mid"] = zg.middle
    ops["zf mid"] = zf.middle

    @op
    def clear():
        oacc[...] = jnp.zeros_like(oacc)
        gacc[...] = jnp.zeros_like(gacc)

    @op
    def zf_end():
        zf.finish()
        values = wide(fg).astype(F32)
        packed = row_pack(
            jnp.sum(values, 0, keepdims=True), jnp.sum(values * values, 0, keepdims=True)
        )
        held["ex"] = exchange(k, k.xs, k.xd, s["stx"], packed)

    @op
    def zg_end():
        zg.finish()
        gw[...] = mmt(identity(TOK), wide(gg)).astype(BF16)

    @op
    def stat_y():
        held["ey"] = exchange(k, k.ys, k.yd, s["sty"], collect(held["ex"], s["stx"]))

    @op
    def norm():
        stat = collect(held["ey"], s["sty"])
        average = stat[0:1] / D
        spread = stat[1:2] / D - average * average
        inverse = lax.rsqrt(spread + EPS)
        s["stat"][...] = row_pack(average, inverse)
        s["nT"][...] = ((wide(fg).astype(F32) - average) * inverse).astype(BF16)
        s["normed"][...] = mmt(identity(TOK), s["nT"][...]).astype(BF16)

    def tile_at(base, t):
        return pl.ds(pl.multiple_of(base + t * TILE, TILE), TILE)

    def head_cols(t):
        return pl.ds(pl.multiple_of(t * 3 * HS, 3 * HS), 3 * HS)

    def product(name, fn, n):
        part = s[name + "0"]

        def run():
            def body(t):
                part[:, :, cols(t)] = fn(t).astype(BF16).reshape(4, 128, TILE)

            tiles(n, body)

        ops["M " + name] = run

    def back(base):
        return lambda t: mmt(gw[...], s["wdown"][tile_at(base, t), :])

    def forth(base):
        return lambda t: mm(s["normed"][...], s["wup"][:, tile_at(base, t)])

    product("Ba", lambda t: mmt(gw[...], s["wout"][...]), 1)
    product("Bh1", back(0), 2)
    product("Bh2", back(1536), 2)
    product("Fh1", forth(0), 2)
    product("Fh2", forth(1536), 2)

    def product_query():
        def body(h):
            s["Fq0"][:, :, head_cols(h)] = (
                mm(s["normed"][...], s["wqkv"][h]).astype(BF16).reshape(4, 128, 3 * HS)
            )

        tiles(HEADS, body)

    ops["M Fq"] = product_query
    for i in range(2, 6):
        ops["load " + str(i)] = loads[i].wait

    def activate(stream, gather, base):
        for i, value in enumerate(R[stream].fin()):
            G[gather].put(i, gelu_value(value).astype(BF16))
            at = base + i * G[gather].ca
            slope[:, at : at + value.shape[1]] = gelu_slope(value)

    def deactivate(stream, gather, base):
        for i, value in enumerate(R[stream].fin()):
            at = base + i * G[gather].ca
            G[gather].put(i, (value * slope[:, at : at + value.shape[1]]).astype(BF16))

    ops["act Fh1"] = lambda: activate("Fh1", "H1", 0)
    ops["act Fh2"] = lambda: activate("Fh2", "H2", 1536)
    ops["deact Bh1"] = lambda: deactivate("Bh1", "G1", 0)
    ops["deact Bh2"] = lambda: deactivate("Bh2", "G2", 1536)

    @op
    def project():
        ja, jb = R["Fq"].fin()
        s["ja"][...] = ja
        s["jb"][...] = jb.reshape(64, 3 * HS)
        normal, _ = head_norm(s["ja"][:, HS : 2 * HS])
        s["KVa"][k.y, :, 0:HS] = normal.astype(BF16)
        s["KVa"][k.y, :, HS : 2 * HS] = s["ja"][:, 2 * HS :].astype(BF16)
        normal, _ = head_norm(s["jb"][:, HS : 2 * HS])
        s["KVb"][k.x, KV.mine, :, 0:HS] = normal.astype(BF16).reshape(2, 32, HS)
        s["KVb"][k.x, KV.mine, :, HS : 2 * HS] = (
            s["jb"][:, 2 * HS :].astype(BF16).reshape(2, 32, HS)
        )

    @op
    def attend():
        parts = R["Ba"].fin()
        for i, (kv, dk, own) in enumerate(
            ((s["KVa"], s["DKa"], s["ja"]), (s["KVb"], s["DKb"], s["jb"]))
        ):
            shape = kv.shape[:-1] + (HS,)
            q_norm, q_inv = head_norm(own[:, 0:HS])
            q_b = q_norm.astype(BF16)
            keys = kv[..., 0:HS].reshape(TOK, HS)
            values = kv[..., HS : 2 * HS].reshape(TOK, HS)
            raised = jnp.exp(mmt(q_b, keys) * FACTOR)
            probs = raised / jnp.sum(raised, -1, keepdims=True)
            probs_b = probs.astype(BF16)
            part = parts[i].astype(BF16).reshape(own.shape[0], HS)
            grad_probs = mmt(part, values)
            row_dot = jnp.sum(probs * grad_probs, -1, keepdims=True)
            grad_scores = (probs * (grad_probs - row_dot)).astype(BF16)
            dk[..., 0:HS] = (mtm(grad_scores, q_b) * FACTOR).astype(BF16).reshape(shape)
            dk[..., HS : 2 * HS] = mtm(probs_b, part).astype(BF16).reshape(shape)
            G["AT"].put_head(i, 0, mm(probs_b, values).astype(BF16))
            grad_query = mm(grad_scores, keys) * FACTOR
            G["GJ"].put_head(i, 0, head_norm_back(grad_query, q_norm, q_inv).astype(BF16))

    def key_value_back(i, own, value):
        k_norm, k_inv = head_norm(own[:, HS : 2 * HS])
        G["GJ"].put_head(i, HS, head_norm_back(value[:, 0:HS], k_norm, k_inv).astype(BF16))
        G["GJ"].put_head(i, 2 * HS, value[:, HS:].astype(BF16))

    ops["KV d3"] = lambda: key_value_back(0, s["ja"], KV.d3())
    ops["KV d4"] = lambda: key_value_back(1, s["jb"], KV.d4().reshape(64, 2 * HS))

    copies = []
    shares = []

    def share(stage, own_out, got_out, index):
        slot = 6 + len(copies)
        mine = pltpu.make_async_copy(stage.at[core, *index], own_out.at[index], local.at[slot])
        mine.start()
        copies.append(mine)
        shares.append(k.send(stage.at[1 - core, *index], got_out.at[index], k.cd))

    def rows_tile(name, t):
        return s[name][:, :, cols(t)].reshape(TOK, TILE)

    def per_tile(name, body, n):
        ops[name] = lambda: tiles(n, body)

    def with_hidden(name, base):
        def total(t):
            oacc[...] += mm(rows_tile(name, t), s["wdown"][tile_at(base, t), :])

        def weights(t):
            both = mm(wide(gg), rows_tile(name, t)).astype(BF16)
            s["sdown"][0, :, tile_at(base, t)] = both[0:192]
            s["sdown"][1, :, tile_at(base, t)] = both[192:384]

        def run():
            tiles(2, weights)
            share(s["sdown"], own_down, got_down, (every, pl.ds(base, 1536)))

        per_tile("acc " + name, total, 2)
        ops["dw " + name] = run

    def with_grads(name, base):
        def total(t):
            gacc[...] += mmt(rows_tile(name, t), s["wup"][:, tile_at(base, t)])

        def weights(t):
            both = mm(s["nT"][...], rows_tile(name, t)).astype(BF16)
            s["sup"][0, :, tile_at(base, t)] = both[0:192]
            s["sup"][1, :, tile_at(base, t)] = both[192:384]

        def run():
            tiles(2, weights)
            share(s["sup"], own_up, got_up, (every, pl.ds(base, 1536)))

        per_tile("acc " + name, total, 2)
        ops["dw " + name] = run

    with_hidden("H1", 0)
    with_hidden("H2", 1536)
    with_grads("G1", 0)
    with_grads("G2", 1536)

    def total_attended(t):
        oacc[...] += mm(rows_tile("AT", 0), s["wout"][...])

    def total_joined(h):
        gacc[...] += mmt(s["GJ"][:, :, head_cols(h)].reshape(TOK, 3 * HS), s["wqkv"][h])

    per_tile("acc AT", total_attended, 1)
    per_tile("acc GJ", total_joined, HEADS)

    def weights_attended():
        both = mm(wide(gg), rows_tile("AT", 0)).astype(BF16)
        for c in range(2):
            for h in range(HEADS):
                s["sattn"][c, h] = both[c * 192 : (c + 1) * 192, h * HS : (h + 1) * HS]
        share(s["sattn"], own_attn, got_attn, (every, every, every))

    ops["dw AT"] = weights_attended

    def zscatter(i, total):
        part = s["zp"].at[i]
        turned = mmt(identity(BLK), total.astype(BF16))
        part[...] = turned.astype(BF16).reshape(4, ZC, TOK)
        ring = RingSum(
            k, k.zs, k.zd, lambda j: part.at[j], *split_rows(48), s["zo"].at[i], s["zn"].at[i]
        )
        return ring, turned

    @op
    def gin():
        average, inverse = s["stat"][0:1], s["stat"][1:2]
        held["zi"], turned = zscatter(1, gacc[...])
        held["zi"].start()
        normal = (wide(fg).astype(F32) - average) * inverse
        packed = row_pack(
            jnp.sum(turned, 0, keepdims=True), jnp.sum(turned * normal, 0, keepdims=True)
        )
        held["bz"] = exchange(k, k.zs, k.zd, s["btz"], packed)

    def weights_joined():
        def body(h):
            block = s["GJ"][:, :, head_cols(h)].reshape(TOK, 3 * HS)
            both = mm(s["nT"][...], block).astype(BF16)
            s["sqkv"][0, h] = both[0:192]
            s["sqkv"][1, h] = both[192:384]

        tiles(HEADS, body)
        share(s["sqkv"], own_qkv, got_qkv, (every, every, every))

    ops["dw GJ"] = weights_joined

    @op
    def zi_mid():
        held["zi"].middle()

    @op
    def back_x():
        held["bx"] = exchange(k, k.xs, k.xd, s["btx"], collect(held["bz"], s["btz"]))

    @op
    def back_y():
        held["by"] = exchange(k, k.ys, k.yd, s["bty"], collect(held["bx"], s["btx"]))

    @op
    def gin_out():
        average, inverse = s["stat"][0:1], s["stat"][1:2]
        summed = held["zi"].total()
        sums = collect(held["by"], s["bty"])
        normal_own = (fg[z].astype(F32) - average) * inverse
        correction = summed - sums[0:1] / D - normal_own * (sums[1:2] / D)
        gin_o[...] = (gg[z].astype(F32) + inverse * correction).astype(BF16)

    @op
    def zl_start():
        held["zl"], _ = zscatter(0, oacc[...])
        held["zl"].start()

    @op
    def zl_mid():
        held["zl"].middle()

    @op
    def layer_out():
        layer_o[...] = (fg[z].astype(F32) + held["zl"].total()).astype(BF16)

    for i, name in enumerate(ORDER):
        ops[name]()
        k.settle(i)

    for copy in copies:
        copy.wait()
    for copy in shares:
        copy.wait_recv()
    k.settle(len(ORDER) + SETTLE)


def on_device(features, w_qkv, w_up, w_out, w_down, grad_out):
    out_flat = w_out.reshape(768, BLK)
    shapes = scratch()
    any_spec = pl.BlockSpec(memory_space=pl.ANY)
    vmem_spec = pl.BlockSpec(memory_space=pltpu.VMEM)

    def pair(*shape):
        return [jax.ShapeDtypeStruct(shape, BF16)] * 2

    names = tuple(shapes)
    outs = pl.pallas_call(
        lambda *refs: kernel(names, *refs),
        out_shape=pair(ZC, TOK)
        + pair(HEADS, 192, 3 * HS)
        + pair(192, 3072)
        + pair(HEADS, 192, HS)
        + pair(192, 3072),
        in_specs=[any_spec] * 6,
        out_specs=[vmem_spec] * 2 + [any_spec] * 8,
        scratch_shapes=list(shapes.values()),
        compiler_params=pltpu.CompilerParams(
            collective_id=0, has_side_effects=True, vmem_limit_bytes=60 * 1024 * 1024
        ),
        cost_estimate=pl.CostEstimate(
            flops=11_000_000_000, bytes_accessed=20_000_000, transcendentals=1_000_000
        ),
    )(features.T, grad_out.T, w_qkv.transpose(1, 0, 2), w_up, out_flat, w_down)

    def both(i):
        return outs[i].astype(F32) + outs[i + 1].astype(F32)

    return (
        outs[0].T,
        outs[1].T,
        both(2).transpose(1, 0, 2),
        both(4),
        both(6).transpose(0, 2, 1),
        both(8).T,
    )


def solution(mesh):
    in_specs = (
        P("dp", ("mx", "my")),
        P("mx", "my", None),
        P("mx", "my"),
        P("my", None, "mx"),
        P("my", "mx"),
        P("dp", ("mx", "my")),
    )
    out_specs = (
        P("dp", ("mx", "my")),
        P("dp", ("mx", "my")),
        P(("mx", "dp"), "my", None),
        P(("mx", "dp"), "my"),
        P("my", None, ("mx", "dp")),
        P("my", ("mx", "dp")),
    )
    return jax.shard_map(
        on_device, mesh=mesh, in_specs=in_specs, out_specs=out_specs, check_vma=False
    )
```

time: 187 us -> 163 us (0.87)
  local copies, waits for them, and re-layouts: 18.3 us -> 1.3 us
  Pallas kernels: 164 us -> 153 us
  other arithmetic: 3.44 us -> 8.02 us
    unnamed x19 -> x14, local copies, waits for them, and re-layouts: 14.7 us -> 1.3 us
    pallas_call x1, Pallas kernels: 164 us -> 153 us  [on_device(): pl.pallas_call(lambda *refs: kernel(names, *refs), out_shape=pair(ZC, TOK...]
    transpose x0 -> x3, other arithmetic: none -> 8.02 us  [the longest x1 3.04 us: on_device(): both(8)]
    reshape x2 -> x0, local copies, waits for them, and re-layouts: 3.66 us -> none  [the longest x1 2.34 us: on_device(): qkv_flat = w_qkv.reshape(BLK, 2304)]
    add x4 -> x0, other arithmetic: 3.44 us -> none  [both(): return outs[i].astype(F32) + outs[i + 1].astype(F32)]
where the time goes in v2:
time: 163 us
  Pallas kernels  153 us (94%)
  other arithmetic  8.02 us (5%)
    pallas_call x1, Pallas kernels, on_device(): pl.pallas_call(lambda *refs: kernel(names, *refs), out_shape=pair(ZC, TOK...  153 us

profile of v2, /device:TPU:0, one launch (start us, length us, event | category | flops | bytes accessed | tf_op | source)
XLA Modules:
  0.0 162.5 jit_solution(7199437874324030279)
XLA Ops:
  0.6 152.5 %shard_map.109 = (bf16[96,512]{1,0:T(8,128)(2,1)}, bf16[96,512]{1,0:T(8,128)(2,1)}, bf16[6,192,384]{2,1,0:T(8,128)(2,1)}, bf16[6,192,384]{2,1,0:T(8,128)(2,1)}, ...) custom-call(bf16[96,512]{1,0:T(8,128)(2,1)} %bitcast.16, ...), custom_call_target="tpu_custom_call" | custom-call | flops 11000000512 | bytes 20000000 | tf_op jit(solution)/shard_map/pallas_call | solution.py:934
  153.2 0.0 copy-start.3
  153.2 2.0 %add_bitcast_fusion.2 = f32[6,128,192]{1,2,0:T(8,128)} fusion(bf16[6,192,128]{2,1,0:T(8,128)(2,1)} %get-tuple-element.23, bf16[6,192,128]{2,1,0:T(8,128)(2,1)} %get-tuple-element.22), kind=kLoop, calls=%fused_computation.3 | loop fusion | flops 442368 | bytes 1179648 | tf_op jit(solution)/shard_map/transpose | solution.py:960
  155.2 0.0 copy-start
  155.2 0.0 copy-start.1
  155.2 0.0 copy-start.2
  155.2 3.0 %add_bitcast_fusion.1 = f32[192,6,384]{2,0,1:T(8,128)} fusion(bf16[6,192,384]{2,1,0:T(8,128)(2,1)} %get-tuple-element.19, bf16[6,192,384]{2,1,0:T(8,128)(2,1)} %get-tuple-element.18), kind=kLoop, calls=%fused_computation.2 | loop fusion | flops 1327104 | bytes 3538944 | tf_op jit(solution)/shard_map/transpose | solution.py:958
  158.2 0.0 copy-done.3
  158.2 0.0 copy-done
  158.2 0.0 copy-done.1
  158.2 0.0 copy-done.2
  158.2 0.0 copy-start.5
  158.2 0.0 copy-start.4
  158.2 3.0 %add_bitcast_fusion = (f32[3072,192]{0,1:T(8,128)}, f32[192,3072]{1,0:T(8,128)}) fusion(bf16[192,3072]{1,0:T(8,128)(2,1)S(1)} %copy-done.3, bf16[192,3072]{1,0:T(8,128)(2,1)S(1)} %copy-done.2, bf16[192,3072]{1,0:T(8,128)(2,1)S(1)} %copy-done.1, bf16[192,3072]{1,0:T(8,128)(2,1)S(1)} %copy-done), kind=kLoop, calls=%fused_computation | loop fusion | flops 3538944 | bytes 9437184 | tf_op jit(solution)/shard_map/transpose | solution.py:961
  161.2 0.0 copy-done.5
  161.2 0.6 copy.14
  161.9 0.0 copy-done.4
  161.9 0.6 copy.15
Async XLA Ops:
  153.2 5.0 %copy-start.3 = (bf16[192,3072]{1,0:T(8,128)(2,1)S(1)}, bf16[192,3072]{1,0:T(8,128)(2,1)}, u32[]{:S(2)}) copy-start(bf16[192,3072]{1,0:T(8,128)(2,1)} %get-tuple-element.25) | copy-start | bytes 3538948
  155.2 3.0 %copy-start = (bf16[192,3072]{1,0:T(8,128)(2,1)S(1)}, bf16[192,3072]{1,0:T(8,128)(2,1)}, u32[]{:S(2)}) copy-start(bf16[192,3072]{1,0:T(8,128)(2,1)} %get-tuple-element.20) | copy-start | bytes 3538948
  155.2 3.0 %copy-start.1 = (bf16[192,3072]{1,0:T(8,128)(2,1)S(1)}, bf16[192,3072]{1,0:T(8,128)(2,1)}, u32[]{:S(2)}) copy-start(bf16[192,3072]{1,0:T(8,128)(2,1)} %get-tuple-element.21) | copy-start | bytes 3538948
  155.2 3.0 %copy-start.2 = (bf16[192,3072]{1,0:T(8,128)(2,1)S(1)}, bf16[192,3072]{1,0:T(8,128)(2,1)}, u32[]{:S(2)}) copy-start(bf16[192,3072]{1,0:T(8,128)(2,1)} %get-tuple-element.24) | copy-start | bytes 3538948
  158.2 3.1 %copy-start.5 = (bf16[96,512]{1,0:T(8,128)(2,1)S(1)}, bf16[96,512]{1,0:T(8,128)(2,1)}, u32[]{:S(2)}) copy-start(bf16[96,512]{1,0:T(8,128)(2,1)} %get-tuple-element.16) | copy-start | bytes 294916
  158.2 3.7 %copy-start.4 = (bf16[96,512]{1,0:T(8,128)(2,1)S(1)}, bf16[96,512]{1,0:T(8,128)(2,1)}, u32[]{:S(2)}) copy-start(bf16[96,512]{1,0:T(8,128)(2,1)} %get-tuple-element.17) | copy-start | bytes 294916

commit v3 on v2

--- a/solution.py
+++ b/solution.py
@@ -19,7 +19,8 @@
 BLK = 384
 ZC = 96
 FACTOR = 1.0 / math.sqrt(HS)
-N_SEMS = 340
+N_SEND = 75
+N_RECV = 86
 TILE = 768
 SETTLE = 16
 
@@ -69,10 +70,21 @@
     ref[...] = (ref[...].astype(F32) + more[...].astype(F32)).astype(ref.dtype)
 
 
+class Message:
+    def __init__(self, links, copy, way, sems):
+        self.links, self.copy, self.way, self.sems = links, copy, way, sems
+        self.began, self.arrived = links.tick(), None
+
+    def wait_recv(self):
+        self.copy.wait_recv()
+        self.arrived = self.links.tick()
+
+
 class Links:
     def __init__(self, send, recv):
-        self.send_sems, self.recv_sems, self.count, self.started = send, recv, 0, []
-        self.turn = 0
+        self.send_sems, self.recv_sems = send, recv
+        self.log, self.started, self.clock, self.turn = [], [], 0, 0
+        self.free_send, self.used_send, self.last_on = [], 0, []
         mx = lax.axis_index("mx")
         self.x, self.y = lax.rem(mx, 4), lax.div(mx, 4)
         self.z, self.core = lax.axis_index("my"), lax.axis_index("dp")
@@ -80,35 +92,66 @@
         self.xs = [lax.rem(x + i, 4) for i in range(4)]
         self.ys = [lax.rem(y + i, 4) for i in range(4)]
         self.zs = [lax.rem(z + i, 4) for i in range(4)]
-        self.xd = [{"mx": y * 4 + v} for v in self.xs]
-        self.yd = [{"mx": v * 4 + x} for v in self.ys]
-        self.zd = [{"my": v} for v in self.zs]
-        self.cd = {"dp": 1 - self.core}
+        self.xd = [{"mx": y * 4 + v, "way": ("x", i)} for i, v in enumerate(self.xs)]
+        self.yd = [{"mx": v * 4 + x, "way": ("y", i)} for i, v in enumerate(self.ys)]
+        self.zd = [{"my": v, "way": ("z", i)} for i, v in enumerate(self.zs)]
+        self.cd = {"dp": 1 - self.core, "way": ("core", 0)}
+
+    def tick(self):
+        self.clock += 1
+        return self.clock
+
+    def ready(self, last, way):
+        if last.arrived is None:
+            return False
+        back = (way[0], (4 - way[1]) % 4)
+        return any(
+            m.way == back and m.began > last.arrived and m.arrived is not None for m in self.log
+        )
+
+    def take_recv(self, way):
+        for i, last in enumerate(self.last_on):
+            if self.ready(last, way):
+                return i
+        self.last_on.append(None)
+        return len(self.last_on) - 1
 
     def send(self, src, dst, device):
-        i = self.count
-        self.count += 1
+        way = device["way"]
+        to = {axis: v for axis, v in device.items() if axis != "way"}
+        if self.free_send:
+            i = self.free_send.pop(0)
+        else:
+            i = self.used_send
+            self.used_send += 1
+        j = self.take_recv(way)
         copy = pltpu.make_async_remote_copy(
             src_ref=src,
             dst_ref=dst,
             send_sem=self.send_sems.at[i],
-            recv_sem=self.recv_sems.at[i],
-            device_id=device,
+            recv_sem=self.recv_sems.at[j],
+            device_id=to,
             device_id_type=MESH,
         )
         copy.start()
-        self.started.append((self.turn, copy))
-        return copy
+        message = Message(self, copy, way, (i, j))
+        self.last_on[j] = message
+        self.log.append(message)
+        self.started.append((self.turn, message))
+        return message
 
     def settle(self, turn):
         self.turn = turn + 1
         while self.started and self.started[0][0] <= turn - SETTLE:
-            self.started.pop(0)[1].wait_send()
+            message = self.started.pop(0)[1]
+            message.copy.wait_send()
+            self.free_send.append(message.sems[0])
 
     def barrier(self):
         sem = pltpu.get_barrier_semaphore()
         peers = self.xd[1:] + self.yd[1:] + self.zd[1:] + [self.cd]
         for peer in peers:
+            peer = {axis: v for axis, v in peer.items() if axis != "way"}
             pl.semaphore_signal(sem, inc=1, device_id=peer, device_id_type=MESH)
         pl.semaphore_wait(sem, len(peers))
 
@@ -319,7 +362,7 @@
         self.a, self.b, self.da, self.db, self.mid, self.got = a, b, da, db, s["DKm"], s["DKg"]
         self.mine = pl.ds(lax.rem(y, 2) * 2, 2)
         self.other = pl.ds(2 - lax.rem(y, 2) * 2, 2)
-        self.mate = {"mx": (y + 1 - 2 * lax.rem(y, 2)) * 4 + x}
+        self.mate = {"mx": (y + 1 - 2 * lax.rem(y, 2)) * 4 + x, "way": ("mate", 0)}
         self.ga = RingGather(k, k.ys, k.yd, lambda j: a.at[j], *split_rows(64))
         self.gb = RingGather(k, k.xs, k.xd, lambda j: b.at[j], *split_rows(2))
         self.ra = RingSum(
@@ -410,94 +453,101 @@
 
 ORDER = (
     "enter",
+    "zg mid",
     "zf start",
-    "zg mid",
-    "zf mid",
     "zg_end",
+    "load 2",
+    "M Ba",
+    "Ba s1",
     "load 3",
-    "M Bh1",
-    "Bh1 s1",
-    "zf_end",
     "M Bh2",
     "Bh2 s1",
-    "clear",
-    "load 2",
-    "M Ba",
-    "Bh1 s2",
-    "Ba s1",
+    "zf mid",
+    "M Bh1",
+    "zf_end",
+    "Bh2 s2",
     "stat_y",
-    "Bh2 s2",
+    "Bh1 s1",
     "norm",
+    "load 5",
+    "M Fh2",
+    "Fh2 s1",
     "load 4",
     "M Fq",
+    "Bh2 s3",
+    "Fh2 s2",
     "Fq s1",
-    "load 5",
+    "Fh2 s3",
+    "Bh2 s4",
     "M Fh1",
-    "M Fh2",
-    "Bh2 s3",
+    "Fq s2",
+    "clear",
+    "Fh2 s4",
+    "Ba s2",
     "Fh1 s1",
+    "Fq s3",
+    "act Fh2",
+    "Bh1 s2",
+    "deact Bh2",
+    "Fq s4",
+    "Fh1 s2",
+    "G2 s1",
     "Bh1 s3",
-    "Fq s2",
-    "Fh2 s1",
-    "Ba s2",
-    "Bh2 s4",
-    "Fh1 s2",
-    "Bh1 s4",
-    "Fq s3",
-    "Fh2 s2",
-    "Ba s3",
-    "Fh1 s3",
-    "Fq s4",
-    "Fh2 s3",
-    "Fh1 s4",
-    "Ba s4",
     "project",
     "KV s1",
-    "act Fh1",
-    "H1 s1",
-    "deact Bh1",
+    "Fh1 s3",
+    "G2 s2",
     "KV s2",
-    "Fh2 s4",
-    "G1 s1",
-    "H1 s2",
+    "Ba s3",
     "KV s3",
-    "act Fh2",
-    "H1 s3",
+    "Ba s4",
+    "G2 s3",
+    "Fh1 s4",
     "KV fin",
+    "H2 s1",
     "attend",
     "KV d1",
+    "Bh1 s4",
+    "G2 s4",
+    "act Fh1",
+    "KV d2",
+    "H1 s1",
+    "H2 s2",
+    "deact Bh1",
+    "G1 s1",
+    "KV d3",
+    "AT s1",
+    "H1 s2",
     "G1 s2",
-    "deact Bh2",
-    "AT s1",
-    "G2 s1",
-    "H1 s4",
-    "KV d2",
-    "H2 s1",
-    "G1 s3",
-    "AT s2",
-    "G2 s2",
-    "H1 fin",
-    "acc H1",
-    "dw H1",
-    "KV d3",
-    "H2 s2",
     "KV d4",
     "GJ s1",
+    "H1 s3",
+    "G2 fin",
+    "dw G2",
+    "GJ s2",
+    "G1 s3",
+    "H1 s4",
+    "GJ s3",
     "G1 s4",
-    "G2 s3",
+    "H1 fin",
+    "AT s2",
+    "dw H1",
+    "GJ s4",
+    "acc H1",
+    "acc G2",
     "H2 s3",
-    "AT s3",
-    "GJ s2",
     "G1 fin",
     "dw G1",
     "acc G1",
-    "G2 s4",
+    "GJ fin",
+    "AT s3",
+    "acc GJ",
+    "gin",
     "H2 s4",
+    "dw GJ",
     "AT s4",
-    "GJ s3",
-    "G2 fin",
-    "acc G2",
-    "dw G2",
+    "back_x",
+    "zi_mid",
     "H2 fin",
     "acc H2",
     "AT fin",
@@ -505,24 +555,17 @@
     "acc AT",
     "zl_start",
     "dw H2",
-    "GJ s4",
+    "back_y",
     "zl_mid",
+    "gin_out",
     "layer_out",
-    "GJ fin",
-    "acc GJ",
-    "gin",
-    "dw GJ",
-    "zi_mid",
-    "back_x",
-    "back_y",
-    "gin_out",
 )
 
 
 def scratch():
     s = {
-        "send": pltpu.SemaphoreType.DMA((N_SEMS,)),
-        "recv": pltpu.SemaphoreType.DMA((N_SEMS,)),
+        "send": pltpu.SemaphoreType.DMA((N_SEND,)),
+        "recv": pltpu.SemaphoreType.DMA((N_RECV,)),
         "local": pltpu.SemaphoreType.DMA((16,)),
         "wqkv": pltpu.VMEM((HEADS, BLK, 3 * HS), BF16),
         "wup": pltpu.VMEM((BLK, 3072), BF16),
@@ -602,8 +645,26 @@
     def wide(buf):
         return buf[...].reshape(BLK, TOK)
 
-    def ring_z(buf):
-        return RingGather(k, k.zs, k.zd, lambda j: buf.at[j], *split_rows(48))
+    class GatherZ:
+        def __init__(self, buf):
+            self.rings = [
+                RingGather(
+                    k, k.zs, k.zd, lambda j, t=t: buf.at[j, :, pl.ds(t, TOK // 2)], *split_rows(48)
+                )
+                for t in (0, TOK // 2)
+            ]
+
+        def start(self):
+            for ring in self.rings:
+                ring.start()
+
+        def middle(self):
+            for ring in self.rings:
+                ring.middle()
+
+        def finish(self):
+            for ring in self.rings:
+                ring.finish()
 
     R = {}
     for name, ca, cb, w, _ in STREAMS:
@@ -621,7 +682,7 @@
         ops["KV " + step] = getattr(KV, step)
     every = slice(None)
     oacc, gacc, slope = s["oacc"], s["gacc"], s["slope"]
-    zf, zg = ring_z(fg), ring_z(gg)
+    zf, zg = GatherZ(fg), GatherZ(gg)
 
     def op(function):
         ops[function.__name__] = function
@@ -949,17 +1010,75 @@
         ),
     )(features.T, grad_out.T, w_qkv.transpose(1, 0, 2), w_up, out_flat, w_down)
 
-    def both(i):
-        return outs[i].astype(F32) + outs[i + 1].astype(F32)
-
+    layer_out, grad_in, *grads = finish(outs)
+    grad_qkv, grad_up, grad_attn, grad_down = grads
     return (
-        outs[0].T,
-        outs[1].T,
-        both(2).transpose(1, 0, 2),
-        both(4),
-        both(6).transpose(0, 2, 1),
-        both(8).T,
+        layer_out.T,
+        grad_in.T,
+        grad_qkv.transpose(1, 0, 2),
+        grad_up,
+        grad_attn.transpose(0, 2, 1),
+        grad_down.T,
     )
+
+
+PIECES = 3
+
+
+def add_halves(*refs):
+    ins, outs, scr = refs[:10], refs[10:16], refs[16:]
+    own, got, total, sem = scr[0:4], scr[4:8], scr[8:12], scr[12]
+    reads, writes = [], []
+
+    def piece(i, ref, p):
+        if ref.shape[0] == HEADS:
+            return ref.at[pl.ds(p * HEADS // PIECES, HEADS // PIECES)]
+        return ref.at[pl.ds(p * 192 // PIECES, 192 // PIECES)]
+
+    def move(src, dst):
+        copy = pltpu.make_async_copy(src, dst, sem.at[len(reads) + len(writes)])
+        copy.start()
+        return copy
+
+    for i in range(4):
+        for p in range(PIECES):
+            for j, into in enumerate((own, got)):
+                reads.append(move(piece(i, ins[2 + 2 * i + j], p), piece(i, into[i], p)))
+    for i in range(2):
+        reads.append(move(ins[i], scr[13 + i]))
+    turn = iter(reads)
+    for i in range(4):
+        for p in range(PIECES):
+            next(turn).wait()
+            next(turn).wait()
+            into = piece(i, total[i], p)
+            into[...] = piece(i, own[i], p)[...].astype(F32) + piece(i, got[i], p)[...].astype(F32)
+            writes.append(move(into, piece(i, outs[2 + i], p)))
+    for i in range(2):
+        next(turn).wait()
+        writes.append(move(scr[13 + i], outs[i]))
+    for copy in writes:
+        copy.wait()
+
+
+def finish(arrays):
+    grads = arrays[2::2]
+    any_spec = pl.BlockSpec(memory_space=pl.ANY)
+    return pl.pallas_call(
+        add_halves,
+        out_shape=[jax.ShapeDtypeStruct((ZC, TOK), BF16)] * 2
+        + [jax.ShapeDtypeStruct(array.shape, F32) for array in grads],
+        in_specs=[any_spec] * 10,
+        out_specs=[any_spec] * 6,
+        scratch_shapes=[pltpu.VMEM(array.shape, BF16) for array in grads] * 2
+        + [pltpu.VMEM(array.shape, F32) for array in grads]
+        + [pltpu.SemaphoreType.DMA((64,))]
+        + [pltpu.VMEM((ZC, TOK), BF16)] * 2,
+        compiler_params=pltpu.CompilerParams(vmem_limit_bytes=60 * 1024 * 1024),
+        cost_estimate=pl.CostEstimate(
+            flops=2_000_000, bytes_accessed=14_500_000, transcendentals=0
+        ),
+    )(*arrays)
 
 
 def solution(mesh):

time: 163 us -> 147 us (0.902)
  other arithmetic: 8.02 us -> 0 us
  Pallas kernels: 153 us -> 146 us
    pallas_call x1, Pallas kernels: 153 us -> 140 us  [on_device(): pl.pallas_call(lambda *refs: kernel(names, *refs), out_shape=pair(ZC, TOK...]
    transpose x3 -> x0, other arithmetic: 8.02 us -> none  [the longest x1 3.04 us: on_device(): both(8)]
    pallas_call x0 -> x1, Pallas kernels: none -> 6.3 us  [finish(): pl.pallas_call(add_halves, out_shape=[jax.ShapeDtypeStruct((ZC, TOK), BF1...]
where the time goes in v3:
time: 147 us
  Pallas kernels  146 us (99%)
    pallas_call x1, Pallas kernels, on_device(): pl.pallas_call(lambda *refs: kernel(names, *refs), out_shape=pair(ZC, TOK...  140 us
    pallas_call x1, Pallas kernels, finish(): pl.pallas_call(add_halves, out_shape=[jax.ShapeDtypeStruct((ZC, TOK), BF1...  6.3 us

profile of v3, /device:TPU:0, one launch (start us, length us, event | category | flops | bytes accessed | tf_op | source)
XLA Modules:
  0.0 147.0 jit_solution(6757136346920459595)
XLA Ops:
  0.6 139.9 %shard_map.109 = (bf16[96,512]{1,0:T(8,128)(2,1)}, bf16[96,512]{1,0:T(8,128)(2,1)}, bf16[6,192,384]{2,1,0:T(8,128)(2,1)}, bf16[6,192,384]{2,1,0:T(8,128)(2,1)}, ...) custom-call(bf16[96,512]{1,0:T(8,128)(2,1)} %bitcast.14, ...), custom_call_target="tpu_custom_call" | custom-call | flops 11000000512 | bytes 20000000 | tf_op jit(solution)/shard_map/pallas_call | solution.py:995
  140.6 6.3 %shard_map.110 = (bf16[96,512]{1,0:T(8,128)(2,1)}, bf16[96,512]{1,0:T(8,128)(2,1)}, f32[6,192,384]{2,1,0:T(8,128)}, f32[192,3072]{1,0:T(8,128)}, f32[6,192,128]{2,1,0:T(8,128)}, /*index=5*/f32[192,3072]{1,0:T(8,128)}) custom-call(bf16[96,512]{1,0:T(8,128)(2,1)} %get-tuple-element.22.refs_0_, bf16[96,512]{1,0:T(8,128)(2,1)} %get-tuple-element.23.refs_1_, ...), custom_call_target="tpu_custom_call" | custom-call | flops 2000000 | bytes 14500000 | tf_op jit(solution)/shard_map/pallas_call | solution.py:1067

commit v4 on v3

--- a/solution.py
+++ b/solution.py
@@ -19,10 +19,10 @@
 BLK = 384
 ZC = 96
 FACTOR = 1.0 / math.sqrt(HS)
-N_SEND = 75
-N_RECV = 86
+N_SEND = 48
+N_RECV = 88
 TILE = 768
-SETTLE = 16
+SETTLE = 8
 
 
 def mm(a, b):
@@ -161,9 +161,10 @@
 
 
 class RingSum:
-    def __init__(self, links, ring, devices, chunk, first, second, opp, near):
+    def __init__(self, links, ring, devices, chunk, first, second, opp, near, exact=None):
         self.k, self.ring, self.dev = links, ring, devices
         self.chunk, self.first, self.second, self.opp, self.near = chunk, first, second, opp, near
+        self.exact = exact or chunk
 
     def start(self):
         far, left, right = (self.chunk(self.ring[i]) for i in (2, 3, 1))
@@ -175,21 +176,22 @@
             self.k.send(self.first(right), self.first(to_right), self.dev[1]),
         ]
 
+    def relay(self, side, half, slot, arrived):
+        j = self.ring[side]
+        part = half(self.chunk(j))
+        arrived.wait_recv()
+        total = half(self.exact(j))[...].astype(F32) + self.opp[slot].astype(F32)
+        part[...] = total.astype(part.dtype)
+        self.near_copies.append(self.k.send(part, half(self.near.at[slot]), self.dev[side]))
+
     def middle(self):
-        left, right = self.chunk(self.ring[3]), self.chunk(self.ring[1])
-        self.far_left.wait_recv()
-        part = self.first(left)
-        add_to(part, self.opp.at[1])
-        self.near_copies.append(self.k.send(part, self.first(self.near.at[1]), self.dev[3]))
-        self.far_right.wait_recv()
-        part = self.second(right)
-        add_to(part, self.opp.at[0])
-        self.near_copies.append(self.k.send(part, self.second(self.near.at[0]), self.dev[1]))
+        self.relay(3, self.first, 1, self.far_left)
+        self.relay(1, self.second, 0, self.far_right)
 
     def total(self):
         for copy in self.near_copies:
             copy.wait_recv()
-        own = self.chunk(self.ring[0])
+        own = self.exact(self.ring[0])
         return own[...].astype(F32) + self.near[0].astype(F32) + self.near[1].astype(F32)
 
 
@@ -224,22 +226,41 @@
     def __init__(self, links, part, bufs, ca, cb, w):
         k = links
         a, b = pl.ds(0, ca), pl.ds(ca, cb)
-        a1o, a1n, b1o, b1n, a2, b2, a2o, a2n, b2o, b2n = bufs
-        self.mid_a, self.mid_b = a2, b2
+        a1o, a1n, b1o, b1n, a2, b2, a2o, a2n, b2o, b2n, *whole = bufs
+        part_x, a2_x, b2_x = whole or (part, a2, b2)
+        self.mids = ((a2, a2_x), (b2, b2_x))
         if w:
-            a2_chunk, a2_split = (lambda j: a2.at[:, part_of(j, w)]), split_rows(64)
-            b2_chunk, b2_split = (
-                lambda j: b2.at[pl.ds(lax.rem(j, 2) * 2, 2), :, part_of(lax.div(j, 2), w)]
-            ), split_rows(1)
+
+            def a2_chunk(ref):
+                return lambda j: ref.at[:, part_of(j, w)]
+
+            def b2_chunk(ref):
+                return lambda j: ref.at[pl.ds(lax.rem(j, 2) * 2, 2), :, part_of(lax.div(j, 2), w)]
+
+            a2_split, b2_split = split_rows(64), split_rows(1)
         else:
-            a2_chunk, a2_split = (lambda j: a2.at[rows_of(j * 32, 32), :]), split_rows(16)
-            b2_chunk, b2_split = (lambda j: b2.at[j]), split_rows(16)
-        self.a1 = RingSum(k, k.ys, k.yd, lambda j: part.at[j, :, a], *split_rows(64), a1o, a1n)
-        self.b1 = RingSum(
-            k, k.xs, k.xd, lambda j: part.at[:, rows_of(j * 32, 32), b], *split_rows(2), b1o, b1n
-        )
-        self.a2 = RingSum(k, k.xs, k.xd, a2_chunk, *a2_split, a2o, a2n)
-        self.b2 = RingSum(k, k.ys, k.yd, b2_chunk, *b2_split, b2o, b2n)
+
+            def a2_chunk(ref):
+                return lambda j: ref.at[rows_of(j * 32, 32), :]
+
+            def b2_chunk(ref):
+                return lambda j: ref.at[j]
+
+            a2_split = b2_split = split_rows(16)
+
+        def a1_chunk(ref):
+            return lambda j: ref.at[j, :, a]
+
+        def b1_chunk(ref):
+            return lambda j: ref.at[:, rows_of(j * 32, 32), b]
+
+        def ring(axis, devices, chunk, split, opp, near, ref, ref_x):
+            return RingSum(k, axis, devices, chunk(ref), *split, opp, near, chunk(ref_x))
+
+        self.a1 = ring(k.ys, k.yd, a1_chunk, split_rows(64), a1o, a1n, part, part_x)
+        self.b1 = ring(k.xs, k.xd, b1_chunk, split_rows(2), b1o, b1n, part, part_x)
+        self.a2 = ring(k.xs, k.xd, a2_chunk, a2_split, a2o, a2n, a2, a2_x)
+        self.b2 = ring(k.ys, k.yd, b2_chunk, b2_split, b2o, b2n, b2, b2_x)
 
     def s1(self):
         self.a1.start()
@@ -250,10 +271,11 @@
         self.b1.middle()
 
     def s3(self):
-        self.mid_a[...] = self.a1.total().astype(self.mid_a.dtype)
-        self.a2.start()
-        self.mid_b[...] = self.b1.total().astype(self.mid_b.dtype)
-        self.b2.start()
+        for before, after, mids in zip((self.a1, self.b1), (self.a2, self.b2), self.mids):
+            total = before.total()
+            for mid in mids:
+                mid[...] = total.astype(mid.dtype)
+            after.start()
 
     def s4(self):
         self.a2.middle()
@@ -267,29 +289,37 @@
     return pl.ds(pl.multiple_of(j * w, 128), w)
 
 
-def scatter_scratch(ca, cb, w, kind):
+def scatter_scratch(ca, cb, w, exact):
     found = [
         pltpu.VMEM((4, 128, ca + cb), BF16),
         pltpu.VMEM((2, 64, ca), BF16),
         pltpu.VMEM((2, 128, ca), BF16),
         pltpu.VMEM((2, 2, 32, cb), BF16),
         pltpu.VMEM((2, 4, 32, cb), BF16),
-        pltpu.VMEM((128, ca), kind),
-        pltpu.VMEM((4, 32, cb), kind),
+        pltpu.VMEM((128, ca), BF16),
+        pltpu.VMEM((4, 32, cb), BF16),
     ]
     if w:
-        return found + [
-            pltpu.VMEM((2, 64, w), kind),
-            pltpu.VMEM((2, 128, w), kind),
-            pltpu.VMEM((2, 1, 32, w), kind),
-            pltpu.VMEM((2, 2, 32, w), kind),
+        found += [
+            pltpu.VMEM((2, 64, w), BF16),
+            pltpu.VMEM((2, 128, w), BF16),
+            pltpu.VMEM((2, 1, 32, w), BF16),
+            pltpu.VMEM((2, 2, 32, w), BF16),
         ]
-    return found + [
-        pltpu.VMEM((2, 16, ca), kind),
-        pltpu.VMEM((2, 32, ca), kind),
-        pltpu.VMEM((2, 16, cb), kind),
-        pltpu.VMEM((2, 32, cb), kind),
-    ]
+    else:
+        found += [
+            pltpu.VMEM((2, 16, ca), BF16),
+            pltpu.VMEM((2, 32, ca), BF16),
+            pltpu.VMEM((2, 16, cb), BF16),
+            pltpu.VMEM((2, 32, cb), BF16),
+        ]
+    if exact:
+        found += [
+            pltpu.VMEM((4, 128, ca + cb), F32),
+            pltpu.VMEM((128, ca), F32),
+            pltpu.VMEM((4, 32, cb), F32),
+        ]
+    return found
 
 
 class Gather:
@@ -366,9 +396,25 @@
         self.ga = RingGather(k, k.ys, k.yd, lambda j: a.at[j], *split_rows(64))
         self.gb = RingGather(k, k.xs, k.xd, lambda j: b.at[j], *split_rows(2))
         self.ra = RingSum(
-            k, k.ys, k.yd, lambda j: da.at[j], *split_rows(64), s["DKao"], s["DKan"]
+            k,
+            k.ys,
+            k.yd,
+            lambda j: da.at[j],
+            *split_rows(64),
+            s["DKao"],
+            s["DKan"],
+            lambda j: s["DKax"].at[j],
         )
-        self.rb = RingSum(k, k.xs, k.xd, lambda j: db.at[j], *split_rows(2), s["DKbo"], s["DKbn"])
+        self.rb = RingSum(
+            k,
+            k.xs,
+            k.xd,
+            lambda j: db.at[j],
+            *split_rows(2),
+            s["DKbo"],
+            s["DKbn"],
+            lambda j: s["DKbx"].at[j],
+        )
 
     def s1(self):
         own = self.b.at[self.k.x, self.mine]
@@ -434,12 +480,12 @@
 
 
 STREAMS = (
-    ("Ba", 512, 256, HS, F32),
-    ("Bh1", 640, 896, 0, BF16),
-    ("Bh2", 640, 896, 0, BF16),
-    ("Fq", 1536, 768, 3 * HS, F32),
-    ("Fh1", 640, 896, 0, BF16),
-    ("Fh2", 640, 896, 0, BF16),
+    ("Ba", 512, 256, HS, True),
+    ("Bh1", 640, 896, 0, False),
+    ("Bh2", 640, 896, 0, False),
+    ("Fq", 1536, 768, 3 * HS, True),
+    ("Fh1", 640, 896, 0, False),
+    ("Fh2", 640, 896, 0, False),
 )
 GATHERS = (
     ("H1", 640, 896, 0),
@@ -463,101 +509,107 @@
     "M Bh2",
     "Bh2 s1",
     "zf mid",
-    "M Bh1",
     "zf_end",
     "Bh2 s2",
+    "Ba s2",
+    "M Bh1",
     "stat_y",
     "Bh1 s1",
+    "Bh2 s3",
     "norm",
     "load 5",
     "M Fh2",
     "Fh2 s1",
+    "M Fh1",
     "load 4",
     "M Fq",
-    "Bh2 s3",
+    "Fq s1",
+    "Fq s2",
+    "Ba s3",
     "Fh2 s2",
-    "Fq s1",
+    "Bh1 s2",
+    "Ba s4",
+    "Fq s3",
+    "clear",
     "Fh2 s3",
+    "Fq s4",
     "Bh2 s4",
-    "M Fh1",
-    "Fq s2",
-    "clear",
     "Fh2 s4",
-    "Ba s2",
     "Fh1 s1",
-    "Fq s3",
+    "project",
+    "KV s1",
     "act Fh2",
-    "Bh1 s2",
+    "Fh1 s2",
     "deact Bh2",
-    "Fq s4",
-    "Fh1 s2",
     "G2 s1",
     "Bh1 s3",
-    "project",
-    "KV s1",
+    "KV s2",
     "Fh1 s3",
     "G2 s2",
-    "KV s2",
-    "Ba s3",
     "KV s3",
-    "Ba s4",
-    "G2 s3",
+    "Bh1 s4",
+    "H2 s1",
     "Fh1 s4",
     "KV fin",
-    "H2 s1",
+    "G2 s3",
     "attend",
+    "H2 s2",
     "KV d1",
-    "Bh1 s4",
+    "AT s1",
+    "act Fh1",
+    "H1 s1",
+    "KV d2",
     "G2 s4",
-    "act Fh1",
-    "KV d2",
-    "H1 s1",
-    "H2 s2",
     "deact Bh1",
+    "KV d3",
     "G1 s1",
-    "KV d3",
-    "AT s1",
+    "AT s2",
     "H1 s2",
-    "G1 s2",
     "KV d4",
     "GJ s1",
-    "H1 s3",
     "G2 fin",
+    "G1 s2",
+    "H2 s3",
+    "GJ s2",
     "dw G2",
-    "GJ s2",
     "G1 s3",
-    "H1 s4",
+    "H2 s4",
     "GJ s3",
     "G1 s4",
-    "H1 fin",
-    "AT s2",
-    "dw H1",
     "GJ s4",
-    "acc H1",
-    "acc G2",
-    "H2 s3",
+    "H2 fin",
+    "H1 s3",
+    "AT s3",
+    "acc H2",
     "G1 fin",
     "dw G1",
+    "dw H2",
     "acc G1",
     "GJ fin",
-    "AT s3",
+    "acc G2",
     "acc GJ",
     "gin",
-    "H2 s4",
+    "H1 s4",
     "dw GJ",
+    "sum G1",
     "AT s4",
+    "zi_mid",
+    "sum G2",
     "back_x",
-    "zi_mid",
-    "H2 fin",
-    "acc H2",
+    "H1 fin",
+    "dw H1",
+    "acc H1",
     "AT fin",
-    "dw AT",
     "acc AT",
     "zl_start",
-    "dw H2",
+    "sum H2",
+    "dw AT",
     "back_y",
     "zl_mid",
+    "sum H1",
+    "sum GJ",
     "gin_out",
+    "sum AT",
     "layer_out",
 )
 
@@ -583,18 +635,18 @@
         "btz": pltpu.VMEM((4, 2, TOK), F32),
         "stat": pltpu.VMEM((2, TOK), F32),
         "slope": pltpu.VMEM((OWN, 3072), F32),
-        "oacc": pltpu.VMEM((TOK, BLK), F32),
-        "gacc": pltpu.VMEM((TOK, BLK), F32),
         "zp": pltpu.VMEM((2, 4, ZC, TOK), BF16),
         "zo": pltpu.VMEM((2, 2, 48, TOK), BF16),
         "zn": pltpu.VMEM((2, 2, ZC, TOK), BF16),
-        "sdown": pltpu.VMEM((2, 192, 3072), BF16),
         "sattn": pltpu.VMEM((2, HEADS, 192, HS), BF16),
-        "sup": pltpu.VMEM((2, 192, 3072), BF16),
         "sqkv": pltpu.VMEM((2, HEADS, 192, 3 * HS), BF16),
+        "gotdown": pltpu.VMEM((2, 96, 3072), BF16),
+        "gotattn": pltpu.VMEM((HEADS, 192, HS), BF16),
+        "gotup": pltpu.VMEM((2, 96, 3072), BF16),
+        "gotqkv": pltpu.VMEM((HEADS, 192, 3 * HS), BF16),
     }
-    for name, ca, cb, w, kind in STREAMS:
-        for i, item in enumerate(scatter_scratch(ca, cb, w, kind)):
+    for name, ca, cb, w, exact in STREAMS:
+        for i, item in enumerate(scatter_scratch(ca, cb, w, exact)):
             s[name + str(i)] = item
     for name, ca, cb, w in GATHERS:
         s[name] = pltpu.VMEM((4, 128, ca + cb), BF16)
@@ -607,6 +659,8 @@
         ("DKan", (2, 128, 256), BF16),
         ("DKbo", (2, 2, 32, 256), BF16),
         ("DKbn", (2, 4, 32, 256), BF16),
+        ("DKax", (4, 128, 256), F32),
+        ("DKbx", (4, 4, 32, 256), F32),
         ("DKm", (4, 32, 256), F32),
         ("DKg", (2, 32, 256), F32),
         ("ja", (128, 3 * HS), F32),
@@ -618,8 +672,8 @@
 
 def kernel(names, feat, gout, w_qkv, w_up, w_out, w_down, *rest):
     layer_o, gin_o = rest[:2]
-    (own_qkv, got_qkv, own_up, got_up, own_attn, got_attn, own_down, got_down) = rest[2:10]
-    s = dict(zip(names, rest[10:]))
+    sum_qkv, sum_up, sum_attn, sum_down = rest[2:6]
+    s = dict(zip(names, rest[6:]))
     k = Links(s["send"], s["recv"])
     z, core = k.z, k.core
     local = s["local"]
@@ -667,8 +721,8 @@
                 ring.finish()
 
     R = {}
-    for name, ca, cb, w, _ in STREAMS:
-        bufs = [s[name + str(i)] for i in range(1, 11)]
+    for name, ca, cb, w, exact in STREAMS:
+        bufs = [s[name + str(i)] for i in range(1, 14 if exact else 11)]
         R[name] = Scatter(k, s[name + "0"], bufs, ca, cb, w)
     G = {name: Gather(k, s[name], ca, cb, w) for name, ca, cb, w in GATHERS}
     KV = KeyValue(k, s)
@@ -680,8 +734,12 @@
                 ops[name + " " + step] = getattr(stream, step)
     for step in ("s1", "s2", "s3", "fin", "d1", "d2"):
         ops["KV " + step] = getattr(KV, step)
-    every = slice(None)
-    oacc, gacc, slope = s["oacc"], s["gacc"], s["slope"]
+    slope = s["slope"]
+    oacc, gacc = (s["Fq11"].at[:, :, pl.ds(i * BLK, BLK)] for i in range(2))
+
+    def add_rows(ref, value):
+        ref[...] += value.reshape(4, 128, BLK)
+
     zf, zg = GatherZ(fg), GatherZ(gg)
 
     def op(function):
@@ -700,8 +758,8 @@
 
     @op
     def clear():
-        oacc[...] = jnp.zeros_like(oacc)
-        gacc[...] = jnp.zeros_like(gacc)
+        for ref in (oacc, gacc):
+            ref[...] = jnp.zeros(ref.shape, F32)
 
     @op
     def zf_end():
@@ -737,12 +795,15 @@
     def head_cols(t):
         return pl.ds(pl.multiple_of(t * 3 * HS, 3 * HS), 3 * HS)
 
+    def store(name, at, value, n):
+        s[name + "0"][:, :, at] = value.astype(BF16).reshape(4, 128, n)
+        if name + "11" in s:
+            s[name + "11"][:, :, at] = value.reshape(4, 128, n)
+
     def product(name, fn, n):
-        part = s[name + "0"]
-
         def run():
             def body(t):
-                part[:, :, cols(t)] = fn(t).astype(BF16).reshape(4, 128, TILE)
+                store(name, cols(t), fn(t), TILE)
 
             tiles(n, body)
 
@@ -762,9 +823,7 @@
 
     def product_query():
         def body(h):
-            s["Fq0"][:, :, head_cols(h)] = (
-                mm(s["normed"][...], s["wqkv"][h]).astype(BF16).reshape(4, 128, 3 * HS)
-            )
+            store("Fq", head_cols(h), mm(s["normed"][...], s["wqkv"][h]), 3 * HS)
 
         tiles(HEADS, body)
 
@@ -805,8 +864,11 @@
     @op
     def attend():
         parts = R["Ba"].fin()
-        for i, (kv, dk, own) in enumerate(
-            ((s["KVa"], s["DKa"], s["ja"]), (s["KVb"], s["DKb"], s["jb"]))
+        for i, (kv, dk, dk_x, own) in enumerate(
+            (
+                (s["KVa"], s["DKa"], s["DKax"], s["ja"]),
+                (s["KVb"], s["DKb"], s["DKbx"], s["jb"]),
+            )
         ):
             shape = kv.shape[:-1] + (HS,)
             q_norm, q_inv = head_norm(own[:, 0:HS])
@@ -820,8 +882,9 @@
             grad_probs = mmt(part, values)
             row_dot = jnp.sum(probs * grad_probs, -1, keepdims=True)
             grad_scores = (probs * (grad_probs - row_dot)).astype(BF16)
-            dk[..., 0:HS] = (mtm(grad_scores, q_b) * FACTOR).astype(BF16).reshape(shape)
-            dk[..., HS : 2 * HS] = mtm(probs_b, part).astype(BF16).reshape(shape)
+            dk_x[..., 0:HS] = (mtm(grad_scores, q_b) * FACTOR).reshape(shape)
+            dk_x[..., HS : 2 * HS] = mtm(probs_b, part).reshape(shape)
+            dk[...] = dk_x[...].astype(BF16)
             G["AT"].put_head(i, 0, mm(probs_b, values).astype(BF16))
             grad_query = mm(grad_scores, keys) * FACTOR
             G["GJ"].put_head(i, 0, head_norm_back(grad_query, q_norm, q_inv).astype(BF16))
@@ -835,14 +898,38 @@
     ops["KV d4"] = lambda: key_value_back(1, s["jb"], KV.d4().reshape(64, 2 * HS))
 
     copies = []
-    shares = []
-
-    def share(stage, own_out, got_out, index):
-        slot = 6 + len(copies)
-        mine = pltpu.make_async_copy(stage.at[core, *index], own_out.at[index], local.at[slot])
-        mine.start()
-        copies.append(mine)
-        shares.append(k.send(stage.at[1 - core, *index], got_out.at[index], k.cd))
+
+    def share(name, half, got, out):
+        def give():
+            held[name] = k.send(half(1 - core), got, k.cd)
+
+        def add():
+            held[name].wait_recv()
+            mine = half(core)
+            add_to(mine, got)
+            copies.append(pltpu.make_async_copy(mine, out, local.at[6 + len(copies)]))
+            copies[-1].start()
+
+        ops["sum " + name] = add
+        return give
+
+    def share_wide(name, stream, got, out, base):
+        assert ORDER.index("dw " + name) > ORDER.index(stream + " s2") + SETTLE
+        at = pl.ds(base, 1536)
+        part = s[stream + "0"]
+        give = share(
+            name,
+            lambda c: part.at[pl.ds(2 * c, 2), pl.ds(0, 96)],
+            s[got].at[:, :, at],
+            out.at[:, :, at],
+        )
+
+        def put(t, value):
+            for c in range(2):
+                half = value[c * 192 : (c + 1) * 192].astype(BF16)
+                part[2 * c : 2 * c + 2, 0:96, cols(t)] = half.reshape(2, 96, TILE)
+
+        return put, give
 
     def rows_tile(name, t):
         return s[name][:, :, cols(t)].reshape(TOK, TILE)
@@ -850,58 +937,62 @@
     def per_tile(name, body, n):
         ops[name] = lambda: tiles(n, body)
 
-    def with_hidden(name, base):
+    def with_hidden(name, stream, base):
+        put, give = share_wide(name, stream, "gotdown", sum_down, base)
+
         def total(t):
-            oacc[...] += mm(rows_tile(name, t), s["wdown"][tile_at(base, t), :])
+            add_rows(oacc, mm(rows_tile(name, t), s["wdown"][tile_at(base, t), :]))
 
         def weights(t):
-            both = mm(wide(gg), rows_tile(name, t)).astype(BF16)
-            s["sdown"][0, :, tile_at(base, t)] = both[0:192]
-            s["sdown"][1, :, tile_at(base, t)] = both[192:384]
+            put(t, mm(wide(gg), rows_tile(name, t)))
 
         def run():
             tiles(2, weights)
-            share(s["sdown"], own_down, got_down, (every, pl.ds(base, 1536)))
+            give()
 
         per_tile("acc " + name, total, 2)
         ops["dw " + name] = run
 
-    def with_grads(name, base):
+    def with_grads(name, stream, base):
+        put, give = share_wide(name, stream, "gotup", sum_up, base)
+
         def total(t):
-            gacc[...] += mmt(rows_tile(name, t), s["wup"][:, tile_at(base, t)])
+            add_rows(gacc, mmt(rows_tile(name, t), s["wup"][:, tile_at(base, t)]))
 
         def weights(t):
-            both = mm(s["nT"][...], rows_tile(name, t)).astype(BF16)
-            s["sup"][0, :, tile_at(base, t)] = both[0:192]
-            s["sup"][1, :, tile_at(base, t)] = both[192:384]
+            put(t, mm(s["nT"][...], rows_tile(name, t)))
 
         def run():
             tiles(2, weights)
-            share(s["sup"], own_up, got_up, (every, pl.ds(base, 1536)))
+            give()
 
         per_tile("acc " + name, total, 2)
         ops["dw " + name] = run
 
-    with_hidden("H1", 0)
-    with_hidden("H2", 1536)
-    with_grads("G1", 0)
-    with_grads("G2", 1536)
+    with_hidden("H1", "Fh1", 0)
+    with_hidden("H2", "Fh2", 1536)
+    with_grads("G1", "Bh1", 0)
+    with_grads("G2", "Bh2", 1536)
 
     def total_attended(t):
-        oacc[...] += mm(rows_tile("AT", 0), s["wout"][...])
+        add_rows(oacc, mm(rows_tile("AT", 0), s["wout"][...]))
 
     def total_joined(h):
-        gacc[...] += mmt(s["GJ"][:, :, head_cols(h)].reshape(TOK, 3 * HS), s["wqkv"][h])
+        block = s["GJ"][:, :, head_cols(h)].reshape(TOK, 3 * HS)
+        add_rows(gacc, mmt(block, s["wqkv"][h]))
 
     per_tile("acc AT", total_attended, 1)
     per_tile("acc GJ", total_joined, HEADS)
+
+    give_attended = share("AT", lambda c: s["sattn"].at[c], s["gotattn"], sum_attn)
+    give_joined = share("GJ", lambda c: s["sqkv"].at[c], s["gotqkv"], sum_qkv)
 
     def weights_attended():
         both = mm(wide(gg), rows_tile("AT", 0)).astype(BF16)
         for c in range(2):
             for h in range(HEADS):
                 s["sattn"][c, h] = both[c * 192 : (c + 1) * 192, h * HS : (h + 1) * HS]
-        share(s["sattn"], own_attn, got_attn, (every, every, every))
+        give_attended()
 
     ops["dw AT"] = weights_attended
 
@@ -917,7 +1008,7 @@
     @op
     def gin():
         average, inverse = s["stat"][0:1], s["stat"][1:2]
-        held["zi"], turned = zscatter(1, gacc[...])
+        held["zi"], turned = zscatter(1, gacc[...].reshape(TOK, BLK))
         held["zi"].start()
         normal = (wide(fg).astype(F32) - average) * inverse
         packed = row_pack(
@@ -933,7 +1024,7 @@
             s["sqkv"][1, h] = both[192:384]
 
         tiles(HEADS, body)
-        share(s["sqkv"], own_qkv, got_qkv, (every, every, every))
+        give_joined()
 
     ops["dw GJ"] = weights_joined
 
@@ -960,7 +1051,7 @@
 
     @op
     def zl_start():
-        held["zl"], _ = zscatter(0, oacc[...])
+        held["zl"], _ = zscatter(0, oacc[...].reshape(TOK, BLK))
         held["zl"].start()
 
     @op
@@ -977,8 +1068,6 @@
 
     for copy in copies:
         copy.wait()
-    for copy in shares:
-        copy.wait_recv()
     k.settle(len(ORDER) + SETTLE)
 
 
@@ -988,29 +1077,25 @@
     any_spec = pl.BlockSpec(memory_space=pl.ANY)
     vmem_spec = pl.BlockSpec(memory_space=pltpu.VMEM)
 
-    def pair(*shape):
-        return [jax.ShapeDtypeStruct(shape, BF16)] * 2
-
+    grads = ((HEADS, 192, 3 * HS), (2, 96, 3072), (HEADS, 192, HS), (2, 96, 3072))
     names = tuple(shapes)
     outs = pl.pallas_call(
         lambda *refs: kernel(names, *refs),
-        out_shape=pair(ZC, TOK)
-        + pair(HEADS, 192, 3 * HS)
-        + pair(192, 3072)
-        + pair(HEADS, 192, HS)
-        + pair(192, 3072),
+        out_shape=[jax.ShapeDtypeStruct(shape, BF16) for shape in ((ZC, TOK),) * 2 + grads],
         in_specs=[any_spec] * 6,
-        out_specs=[vmem_spec] * 2 + [any_spec] * 8,
+        out_specs=[vmem_spec] * 2 + [any_spec] * 4,
         scratch_shapes=list(shapes.values()),
         compiler_params=pltpu.CompilerParams(
-            collective_id=0, has_side_effects=True, vmem_limit_bytes=60 * 1024 * 1024
+            collective_id=0, has_side_effects=True, vmem_limit_bytes=62 * 1024 * 1024
         ),
         cost_estimate=pl.CostEstimate(
             flops=11_000_000_000, bytes_accessed=20_000_000, transcendentals=1_000_000
         ),
     )(features.T, grad_out.T, w_qkv.transpose(1, 0, 2), w_up, out_flat, w_down)
 
-    layer_out, grad_in, *grads = finish(outs)
+    layer_out, grad_in, *grads = finish(
+        [out.reshape(192, 3072) if out.shape[0] == 2 else out for out in outs]
+    )
     grad_qkv, grad_up, grad_attn, grad_down = grads
     return (
         layer_out.T,
@@ -1025,15 +1110,14 @@
 PIECES = 3
 
 
-def add_halves(*refs):
-    ins, outs, scr = refs[:10], refs[10:16], refs[16:]
-    own, got, total, sem = scr[0:4], scr[4:8], scr[8:12], scr[12]
+def widen_grads(*refs):
+    ins, outs, scr = refs[:6], refs[6:12], refs[12:]
+    narrow, whole, small, sem = scr[0:4], scr[4:8], scr[8:10], scr[10]
     reads, writes = [], []
 
-    def piece(i, ref, p):
-        if ref.shape[0] == HEADS:
-            return ref.at[pl.ds(p * HEADS // PIECES, HEADS // PIECES)]
-        return ref.at[pl.ds(p * 192 // PIECES, 192 // PIECES)]
+    def piece(ref, p):
+        n = ref.shape[0] // PIECES
+        return ref.at[pl.ds(p * n, n)]
 
     def move(src, dst):
         copy = pltpu.make_async_copy(src, dst, sem.at[len(reads) + len(writes)])
@@ -1042,41 +1126,39 @@
 
     for i in range(4):
         for p in range(PIECES):
-            for j, into in enumerate((own, got)):
-                reads.append(move(piece(i, ins[2 + 2 * i + j], p), piece(i, into[i], p)))
+            reads.append(move(piece(ins[2 + i], p), piece(narrow[i], p)))
     for i in range(2):
-        reads.append(move(ins[i], scr[13 + i]))
+        reads.append(move(ins[i], small[i]))
     turn = iter(reads)
     for i in range(4):
         for p in range(PIECES):
             next(turn).wait()
-            next(turn).wait()
-            into = piece(i, total[i], p)
-            into[...] = piece(i, own[i], p)[...].astype(F32) + piece(i, got[i], p)[...].astype(F32)
-            writes.append(move(into, piece(i, outs[2 + i], p)))
+            into = piece(whole[i], p)
+            into[...] = piece(narrow[i], p)[...].astype(F32)
+            writes.append(move(into, piece(outs[2 + i], p)))
     for i in range(2):
         next(turn).wait()
-        writes.append(move(scr[13 + i], outs[i]))
+        writes.append(move(small[i], outs[i]))
     for copy in writes:
         copy.wait()
 
 
 def finish(arrays):
-    grads = arrays[2::2]
+    grads = arrays[2:]
     any_spec = pl.BlockSpec(memory_space=pl.ANY)
     return pl.pallas_call(
-        add_halves,
+        widen_grads,
         out_shape=[jax.ShapeDtypeStruct((ZC, TOK), BF16)] * 2
         + [jax.ShapeDtypeStruct(array.shape, F32) for array in grads],
-        in_specs=[any_spec] * 10,
+        in_specs=[any_spec] * 6,
         out_specs=[any_spec] * 6,
-        scratch_shapes=[pltpu.VMEM(array.shape, BF16) for array in grads] * 2
+        scratch_shapes=[pltpu.VMEM(array.shape, BF16) for array in grads]
         + [pltpu.VMEM(array.shape, F32) for array in grads]
-        + [pltpu.SemaphoreType.DMA((64,))]
-        + [pltpu.VMEM((ZC, TOK), BF16)] * 2,
+        + [pltpu.VMEM((ZC, TOK), BF16)] * 2
+        + [pltpu.SemaphoreType.DMA((8 * PIECES + 4,))],
         compiler_params=pltpu.CompilerParams(vmem_limit_bytes=60 * 1024 * 1024),
         cost_estimate=pl.CostEstimate(
-            flops=2_000_000, bytes_accessed=14_500_000, transcendentals=0
+            flops=2_000_000, bytes_accessed=11_000_000, transcendentals=0
         ),
     )(*arrays)
 

time: 147 us -> 142 us (0.966)
  Pallas kernels: 146 us -> 141 us
    pallas_call x2, Pallas kernels: 146 us -> 141 us  [the longest x1 137 us: on_device(): pl.pallas_call(lambda *refs: kernel(names, *refs), out_shape=[jax.ShapeDt...]
where the time goes in v4:
time: 142 us
  Pallas kernels  141 us (99%)
    pallas_call x1, Pallas kernels, on_device(): pl.pallas_call(lambda *refs: kernel(names, *refs), out_shape=[jax.ShapeDt...  137 us
    pallas_call x1, Pallas kernels, finish(): pl.pallas_call(widen_grads, out_shape=[jax.ShapeDtypeStruct((ZC, TOK), BF...  4.17 us

profile of v4, /device:TPU:0, one launch (start us, length us, event | category | flops | bytes accessed | tf_op | source)
XLA Modules:
  0.0 141.6 jit_solution(6063671900981877835)
XLA Ops:
  0.6 136.6 %shard_map.109 = (bf16[96,512]{1,0:T(8,128)(2,1)}, bf16[96,512]{1,0:T(8,128)(2,1)}, bf16[6,192,384]{2,1,0:T(8,128)(2,1)}, bf16[2,96,3072]{2,1,0:T(8,128)(2,1)}, ...) custom-call(bf16[96,512]{1,0:T(8,128)(2,1)} %bitcast.18, bf16[96,512]{1,0:T(8,128)(2,1)} %bitcast.19, ...), custom_call_target="tpu_custom_call" | custom-call | flops 11000000512 | bytes 20000000 | tf_op jit(solution)/shard_map/pallas_call | solution.py:1082
  137.3 4.2 %shard_map.110 = (bf16[96,512]{1,0:T(8,128)(2,1)}, bf16[96,512]{1,0:T(8,128)(2,1)}, f32[6,192,384]{2,1,0:T(8,128)}, f32[192,3072]{1,0:T(8,128)}, f32[6,192,128]{2,1,0:T(8,128)}, /*index=5*/f32[192,3072]{1,0:T(8,128)}) custom-call(bf16[96,512]{1,0:T(8,128)(2,1)} %get-tuple-element.18.refs_0_, bf16[96,512]{1,0:T(8,128)(2,1)} %get-tuple-element.19.refs_1_, ...), custom_call_target="tpu_custom_call" | custom-call | flops 2000000 | bytes 11000000 | tf_op jit(solution)/shard_map/pallas_call | solution.py:1149

commit v5 on v4

--- a/solution.py
+++ b/solution.py
@@ -19,8 +19,8 @@
 BLK = 384
 ZC = 96
 FACTOR = 1.0 / math.sqrt(HS)
-N_SEND = 48
-N_RECV = 88
+N_SEND = 52
+N_RECV = 91
 TILE = 768
 SETTLE = 8
 
@@ -452,10 +452,8 @@
 
 
 def tiles(n, body):
-    if n == 1:
-        body(0)
-    else:
-        pl.loop(0, n)(body)
+    for t in range(n):
+        body(t)
 
 
 def cols(t):
@@ -515,86 +513,85 @@
     "M Bh1",
     "stat_y",
     "Bh1 s1",
-    "Bh2 s3",
     "norm",
     "load 5",
     "M Fh2",
     "Fh2 s1",
-    "M Fh1",
     "load 4",
     "M Fq",
     "Fq s1",
+    "Fh2 s2",
+    "Ba s3",
     "Fq s2",
-    "Ba s3",
-    "Fh2 s2",
+    "M Fh1",
+    "Bh2 s3",
+    "Fh2 s3",
     "Bh1 s2",
+    "Fq s3",
+    "Fh2 s4",
+    "Bh2 s4",
     "Ba s4",
-    "Fq s3",
-    "clear",
-    "Fh2 s3",
     "Fq s4",
-    "Bh2 s4",
-    "Fh2 s4",
     "Fh1 s1",
+    "act Fh2",
+    "deact Bh2",
+    "G2 s1",
     "project",
     "KV s1",
-    "act Fh2",
     "Fh1 s2",
-    "deact Bh2",
-    "G2 s1",
+    "KV s2",
+    "G2 s2",
+    "H2 s1",
     "Bh1 s3",
-    "KV s2",
+    "KV s3",
     "Fh1 s3",
-    "G2 s2",
-    "KV s3",
+    "G2 s3",
+    "KV fin",
+    "attend",
+    "KV d1",
+    "H2 s2",
+    "Fh1 s4",
     "Bh1 s4",
-    "H2 s1",
-    "Fh1 s4",
-    "KV fin",
-    "G2 s3",
-    "attend",
-    "H2 s2",
-    "KV d1",
+    "KV d2",
+    "H2 s3",
+    "act Fh1",
+    "KV d3",
+    "deact Bh1",
+    "H1 s1",
+    "G1 s1",
+    "KV d4",
+    "H2 s4",
+    "GJ s1",
+    "G1 s2",
+    "G2 s4",
+    "H1 s2",
+    "GJ s2",
+    "G1 s3",
     "AT s1",
-    "act Fh1",
-    "H1 s1",
-    "KV d2",
-    "G2 s4",
-    "deact Bh1",
-    "KV d3",
-    "G1 s1",
+    "GJ s3",
+    "clear",
+    "G1 s4",
+    "G2 fin",
+    "acc G2",
+    "dw G2",
     "AT s2",
-    "H1 s2",
-    "KV d4",
-    "GJ s1",
-    "G2 fin",
-    "G1 s2",
-    "H2 s3",
-    "GJ s2",
-    "dw G2",
-    "G1 s3",
-    "H2 s4",
-    "GJ s3",
-    "G1 s4",
     "GJ s4",
+    "H1 s3",
     "H2 fin",
-    "H1 s3",
+    "G1 fin",
+    "acc G1",
+    "dw G1",
     "AT s3",
-    "acc H2",
-    "G1 fin",
-    "dw G1",
     "dw H2",
-    "acc G1",
     "GJ fin",
-    "acc G2",
     "acc GJ",
     "gin",
+    "acc H2",
     "H1 s4",
     "dw GJ",
-    "sum G1",
+    "sum G2",
+    "zi_mid",
     "AT s4",
-    "zi_mid",
-    "sum G2",
     "back_x",
     "H1 fin",
     "dw H1",
@@ -603,12 +600,13 @@
     "acc AT",
     "zl_start",
     "sum H2",
+    "sum G1",
     "dw AT",
     "back_y",
     "zl_mid",
-    "sum H1",
     "sum GJ",
     "gin_out",
+    "sum H1",
     "sum AT",
     "layer_out",
 )
@@ -618,8 +616,8 @@
     s = {
         "send": pltpu.SemaphoreType.DMA((N_SEND,)),
         "recv": pltpu.SemaphoreType.DMA((N_RECV,)),
-        "local": pltpu.SemaphoreType.DMA((16,)),
-        "wqkv": pltpu.VMEM((HEADS, BLK, 3 * HS), BF16),
+        "local": pltpu.SemaphoreType.DMA((17,)),
+        "wqkv": pltpu.VMEM((BLK, HEADS * 3 * HS), BF16),
         "wup": pltpu.VMEM((BLK, 3072), BF16),
         "wout": pltpu.VMEM((768, BLK), BF16),
         "wdown": pltpu.VMEM((3072, BLK), BF16),
@@ -687,8 +685,10 @@
                 (feat, fg.at[z]),
                 (w_out, s["wout"]),
                 (w_down, s["wdown"]),
-                (w_qkv, s["wqkv"]),
                 (w_up, s["wup"]),
+            )
+            + tuple(
+                (w_qkv.at[h], s["wqkv"].at[:, pl.ds(h * 3 * HS, 3 * HS)]) for h in range(HEADS)
             )
         )
     ]
@@ -792,9 +792,6 @@
     def tile_at(base, t):
         return pl.ds(pl.multiple_of(base + t * TILE, TILE), TILE)
 
-    def head_cols(t):
-        return pl.ds(pl.multiple_of(t * 3 * HS, 3 * HS), 3 * HS)
-
     def store(name, at, value, n):
         s[name + "0"][:, :, at] = value.astype(BF16).reshape(4, 128, n)
         if name + "11" in s:
@@ -821,15 +818,15 @@
     product("Fh1", forth(0), 2)
     product("Fh2", forth(1536), 2)
 
-    def product_query():
-        def body(h):
-            store("Fq", head_cols(h), mm(s["normed"][...], s["wqkv"][h]), 3 * HS)
-
-        tiles(HEADS, body)
-
-    ops["M Fq"] = product_query
-    for i in range(2, 6):
-        ops["load " + str(i)] = loads[i].wait
+    product("Fq", lambda t: mm(s["normed"][...], s["wqkv"][:, cols(t)]), 3)
+
+    @op
+    def load_query():
+        for load in loads[5:]:
+            load.wait()
+
+    ops["load 2"], ops["load 3"], ops["load 5"] = (loads[i].wait for i in (2, 3, 4))
+    ops["load 4"] = load_query
 
     def activate(stream, gather, base):
         for i, value in enumerate(R[stream].fin()):
@@ -907,7 +904,7 @@
             held[name].wait_recv()
             mine = half(core)
             add_to(mine, got)
-            copies.append(pltpu.make_async_copy(mine, out, local.at[6 + len(copies)]))
+            copies.append(pltpu.make_async_copy(mine, out, local.at[11 + len(copies)]))
             copies[-1].start()
 
         ops["sum " + name] = add
@@ -934,14 +931,14 @@
     def rows_tile(name, t):
         return s[name][:, :, cols(t)].reshape(TOK, TILE)
 
-    def per_tile(name, body, n):
-        ops[name] = lambda: tiles(n, body)
+    def whole(name):
+        return s[name][...].reshape(TOK, s[name].shape[2])
 
     def with_hidden(name, stream, base):
         put, give = share_wide(name, stream, "gotdown", sum_down, base)
 
-        def total(t):
-            add_rows(oacc, mm(rows_tile(name, t), s["wdown"][tile_at(base, t), :]))
+        def total():
+            add_rows(oacc, mm(whole(name), s["wdown"][pl.ds(base, 1536), :]))
 
         def weights(t):
             put(t, mm(wide(gg), rows_tile(name, t)))
@@ -950,14 +947,14 @@
             tiles(2, weights)
             give()
 
-        per_tile("acc " + name, total, 2)
+        ops["acc " + name] = total
         ops["dw " + name] = run
 
     def with_grads(name, stream, base):
         put, give = share_wide(name, stream, "gotup", sum_up, base)
 
-        def total(t):
-            add_rows(gacc, mmt(rows_tile(name, t), s["wup"][:, tile_at(base, t)]))
+        def total():
+            add_rows(gacc, mmt(whole(name), s["wup"][:, pl.ds(base, 1536)]))
 
         def weights(t):
             put(t, mm(s["nT"][...], rows_tile(name, t)))
@@ -966,7 +963,7 @@
             tiles(2, weights)
             give()
 
-        per_tile("acc " + name, total, 2)
+        ops["acc " + name] = total
         ops["dw " + name] = run
 
     with_hidden("H1", "Fh1", 0)
@@ -974,15 +971,8 @@
     with_grads("G1", "Bh1", 0)
     with_grads("G2", "Bh2", 1536)
 
-    def total_attended(t):
-        add_rows(oacc, mm(rows_tile("AT", 0), s["wout"][...]))
-
-    def total_joined(h):
-        block = s["GJ"][:, :, head_cols(h)].reshape(TOK, 3 * HS)
-        add_rows(gacc, mmt(block, s["wqkv"][h]))
-
-    per_tile("acc AT", total_attended, 1)
-    per_tile("acc GJ", total_joined, HEADS)
+    ops["acc AT"] = lambda: add_rows(oacc, mm(whole("AT"), s["wout"][...]))
+    ops["acc GJ"] = lambda: add_rows(gacc, mmt(whole("GJ"), s["wqkv"][...]))
 
     give_attended = share("AT", lambda c: s["sattn"].at[c], s["gotattn"], sum_attn)
     give_joined = share("GJ", lambda c: s["sqkv"].at[c], s["gotqkv"], sum_qkv)
@@ -1017,13 +1007,13 @@
         held["bz"] = exchange(k, k.zs, k.zd, s["btz"], packed)
 
     def weights_joined():
-        def body(h):
-            block = s["GJ"][:, :, head_cols(h)].reshape(TOK, 3 * HS)
-            both = mm(s["nT"][...], block).astype(BF16)
-            s["sqkv"][0, h] = both[0:192]
-            s["sqkv"][1, h] = both[192:384]
-
-        tiles(HEADS, body)
+        for t in range(3):
+            both = mm(s["nT"][...], rows_tile("GJ", t)).astype(BF16)
+            for c in range(2):
+                for i in range(2):
+                    s["sqkv"][c, 2 * t + i] = both[
+                        c * 192 : (c + 1) * 192, i * 3 * HS : (i + 1) * 3 * HS
+                    ]
         give_joined()
 
     ops["dw GJ"] = weights_joined

time: 142 us -> 141 us (level)
  no operation moved by 1% of the time
where the time goes in v5:
time: 141 us
  Pallas kernels  140 us (99%)
    pallas_call x1, Pallas kernels, on_device(): pl.pallas_call(lambda *refs: kernel(names, *refs), out_shape=[jax.ShapeDt...  136 us
    pallas_call x1, Pallas kernels, finish(): pl.pallas_call(widen_grads, out_shape=[jax.ShapeDtypeStruct((ZC, TOK), BF...  4.17 us

profile of v5, /device:TPU:0, one launch (start us, length us, event | category | flops | bytes accessed | tf_op | source)
XLA Modules:
  0.0 140.5 jit_solution(4062880434052959450)
XLA Ops:
  0.6 135.5 %shard_map.109 = (bf16[96,512]{1,0:T(8,128)(2,1)}, bf16[96,512]{1,0:T(8,128)(2,1)}, bf16[6,192,384]{2,1,0:T(8,128)(2,1)}, bf16[2,96,3072]{2,1,0:T(8,128)(2,1)}, ...) custom-call(bf16[96,512]{1,0:T(8,128)(2,1)} %bitcast.18, bf16[96,512]{1,0:T(8,128)(2,1)} %bitcast.19, ...), custom_call_target="tpu_custom_call" | custom-call | flops 11000000512 | bytes 20000000 | tf_op jit(solution)/shard_map/pallas_call | solution.py:1072
  136.2 4.2 %shard_map.110 = (bf16[96,512]{1,0:T(8,128)(2,1)}, bf16[96,512]{1,0:T(8,128)(2,1)}, f32[6,192,384]{2,1,0:T(8,128)}, f32[192,3072]{1,0:T(8,128)}, f32[6,192,128]{2,1,0:T(8,128)}, /*index=5*/f32[192,3072]{1,0:T(8,128)}) custom-call(bf16[96,512]{1,0:T(8,128)(2,1)} %get-tuple-element.18.refs_0_, bf16[96,512]{1,0:T(8,128)(2,1)} %get-tuple-element.19.refs_1_, ...), custom_call_target="tpu_custom_call" | custom-call | flops 2000000 | bytes 11000000 | tf_op jit(solution)/shard_map/pallas_call | solution.py:1139

commit v6 on v5

--- a/solution.py
+++ b/solution.py
@@ -623,6 +623,7 @@
         "wdown": pltpu.VMEM((3072, BLK), BF16),
         "fg": pltpu.VMEM((4, ZC, TOK), BF16),
         "gg": pltpu.VMEM((4, ZC, TOK), BF16),
+        "eye": pltpu.VMEM((TOK, TOK), BF16),
         "gw": pltpu.VMEM((TOK, BLK), BF16),
         "normed": pltpu.VMEM((TOK, BLK), BF16),
         "nT": pltpu.VMEM((BLK, TOK), BF16),
@@ -750,6 +751,7 @@
     def enter():
         loads[0].wait()
         zg.start()
+        s["eye"][...] = identity(TOK)
         loads[1].wait()
 
     ops["zf start"] = zf.start
@@ -773,7 +775,7 @@
     @op
     def zg_end():
         zg.finish()
-        gw[...] = mmt(identity(TOK), wide(gg)).astype(BF16)
+        gw[...] = mmt(s["eye"][...], wide(gg)).astype(BF16)
 
     @op
     def stat_y():
@@ -787,7 +789,7 @@
         inverse = lax.rsqrt(spread + EPS)
         s["stat"][...] = row_pack(average, inverse)
         s["nT"][...] = ((wide(fg).astype(F32) - average) * inverse).astype(BF16)
-        s["normed"][...] = mmt(identity(TOK), s["nT"][...]).astype(BF16)
+        s["normed"][...] = mmt(s["eye"][...], s["nT"][...]).astype(BF16)
 
     def tile_at(base, t):
         return pl.ds(pl.multiple_of(base + t * TILE, TILE), TILE)
@@ -988,7 +990,7 @@
 
     def zscatter(i, total):
         part = s["zp"].at[i]
-        turned = mmt(identity(BLK), total.astype(BF16))
+        turned = mmt(s["eye"][0:BLK, 0:BLK], total.astype(BF16))
         part[...] = turned.astype(BF16).reshape(4, ZC, TOK)
         ring = RingSum(
             k, k.zs, k.zd, lambda j: part.at[j], *split_rows(48), s["zo"].at[i], s["zn"].at[i]

time: 141 us -> 140 us (level)
  no operation moved by 1% of the time
where the time goes in v6:
time: 140 us
  Pallas kernels  140 us (100%)
    pallas_call x1, Pallas kernels, on_device(): pl.pallas_call(lambda *refs: kernel(names, *refs), out_shape=[jax.ShapeDt...  135 us
    pallas_call x1, Pallas kernels, finish(): pl.pallas_call(widen_grads, out_shape=[jax.ShapeDtypeStruct((ZC, TOK), BF...  4.17 us

profile of v6, /device:TPU:0, one launch (start us, length us, event | category | flops | bytes accessed | tf_op | source)
XLA Modules:
  0.0 140.4 jit_solution(3864973561429606532)
XLA Ops:
  0.6 135.4 %shard_map.109 = (bf16[96,512]{1,0:T(8,128)(2,1)}, bf16[96,512]{1,0:T(8,128)(2,1)}, bf16[6,192,384]{2,1,0:T(8,128)(2,1)}, bf16[2,96,3072]{2,1,0:T(8,128)(2,1)}, ...) custom-call(bf16[96,512]{1,0:T(8,128)(2,1)} %bitcast.18, bf16[96,512]{1,0:T(8,128)(2,1)} %bitcast.19, ...), custom_call_target="tpu_custom_call" | custom-call | flops 11000000512 | bytes 20000000 | tf_op jit(solution)/shard_map/pallas_call | solution.py:1074
  136.0 4.2 %shard_map.110 = (bf16[96,512]{1,0:T(8,128)(2,1)}, bf16[96,512]{1,0:T(8,128)(2,1)}, f32[6,192,384]{2,1,0:T(8,128)}, f32[192,3072]{1,0:T(8,128)}, f32[6,192,128]{2,1,0:T(8,128)}, /*index=5*/f32[192,3072]{1,0:T(8,128)}) custom-call(bf16[96,512]{1,0:T(8,128)(2,1)} %get-tuple-element.18.refs_0_, bf16[96,512]{1,0:T(8,128)(2,1)} %get-tuple-element.19.refs_1_, ...), custom_call_target="tpu_custom_call" | custom-call | flops 2000000 | bytes 11000000 | tf_op jit(solution)/shard_map/pallas_call | solution.py:1141
